TPU v7x, 32 devices: a whole 2x2x4 slice. The times are simulated.
32 devices in a mesh: blk: 16 (over z, y, core), rep: 2 (over x).
Axes of the slice: x: 2, y: 2, z: 4, core: 2. Of those that a mesh axis runs over, the one named last changes fastest.
Arguments:
- samples: bfloat16 [512, 16, 2048], P('blk', 'rep'), may hold values from -60 to 60, as said below
- offsets: int32 [4, 512], P(None, 'blk'), may hold values from 0 to 31
- bad_mask: int32 [512], P('blk'), may hold values 0 or 1
Outputs:
- correlations: float32 [512, 4, 257], P('blk')
- mirrored: float32 [512, 4, 257], P('blk')
Inputs may be any that keep to these rules, and one draw needn't show every extreme that they name: `samples`: samples vary in scale between channels and segments; channels near one another share a delayed common source.
All inputs are finite; a program needn't handle non-finite values. No bound on the sum of `bad_mask` on one device may be relied on, other than what follows from the above.
Results may differ from a plain program's by a relative error of at most 0.0017.
Values may be sent and summed in bfloat16 or wider, within the bound.
A program may use at most 64 MiB of HBM per device.

v0:
```python
import math

import jax
import jax.numpy as jnp
from jax import lax
from jax.sharding import PartitionSpec as P

LAGS = 128


def shifted(x, axis, by):
    length = lax.axis_size(axis)
    return lax.ppermute(x, axis, [(i, (i + by) % length) for i in range(length)])


def forward_table(length):
    half_len = length // 2
    sample_idx = lax.iota(jnp.int32, length)
    bin_idx = lax.iota(jnp.int32, half_len)
    phase = sample_idx[:, None] * bin_idx[None, :] % length
    angle = phase.astype(jnp.float32) * (2.0 * math.pi / length)
    return jnp.concatenate([jnp.cos(angle), -jnp.sin(angle)], axis=1).astype(jnp.bfloat16)


def inverse_table(length, lag_half):
    half_len = length // 2
    bin_idx = lax.iota(jnp.int32, half_len)
    lag_idx = lax.iota(jnp.int32, 2 * lag_half + 1) - lag_half
    phase = bin_idx[:, None] * (lag_idx[None, :] % length) % length
    angle = phase.astype(jnp.float32) * (2.0 * math.pi / length)
    return jnp.concatenate([jnp.cos(angle), -jnp.sin(angle)], axis=0)


def whiten(spectrum, keep, half_len):
    power = jnp.sum(spectrum * spectrum, axis=-1, keepdims=True) / half_len
    return (spectrum * lax.rsqrt(power + 1e-06) * keep[:, None, None]).astype(jnp.bfloat16)


def cross_spectrum(local, partner, half_len):
    first = local.astype(jnp.float32)
    second = partner.astype(jnp.float32)
    real_a, imag_a = (first[..., :half_len], first[..., half_len:])
    real_b, imag_b = (second[..., :half_len], second[..., half_len:])
    real_sum = jnp.sum(real_a * real_b + imag_a * imag_b, axis=1)
    imag_sum = jnp.sum(imag_a * real_b - real_a * imag_b, axis=1)
    return jnp.concatenate([real_sum, imag_sum], axis=-1)


def on_device(samples, offsets, bad_mask):
    channels, segments, length = samples.shape
    half_len = length // 2
    stops = offsets.shape[0]
    spectrum = jnp.dot(
        samples.reshape(channels * segments, length),
        forward_table(length),
        preferred_element_type=jnp.float32,
    ).reshape(channels, segments, length)
    keep = (1 - bad_mask).astype(jnp.float32)
    white = whiten(spectrum, keep, half_len)
    pieces = []
    moving = white
    for stop in range(1, stops + 1):
        moving = shifted(moving, "blk", 1)
        partner = jnp.take(moving, offsets[stop - 1], axis=0)
        pieces.append(cross_spectrum(white, partner, half_len))
    cross = jnp.stack(pieces, axis=1)
    scale = 1.0 / math.sqrt(segments * lax.axis_size("rep") * half_len)
    back_table = inverse_table(length, LAGS)
    stacked = lax.psum(cross, "rep")
    correlations = (
        jnp.dot(
            stacked.reshape(channels * stops, length),
            back_table,
            precision=lax.Precision.HIGHEST,
            preferred_element_type=jnp.float32,
        ).reshape(channels, stops, -1)
        * scale
    )
    mirrored = []
    for stop in range(1, stops + 1):
        flipped = correlations[:, stop - 1, ::-1]
        mirrored.append(shifted(flipped, "blk", -stop))
    return (correlations, jnp.stack(mirrored, axis=1))


def solution(mesh):
    return jax.shard_map(
        on_device,
        mesh=mesh,
        in_specs=(P("blk", "rep", None), P(None, "blk"), P("blk")),
        out_specs=(P("blk", None, None), P("blk", None, None)),
        check_vma=False,
    )
```

profile of v0, /device:TPU:0, one launch (start us, length us, event | category | flops | bytes accessed | tf_op | source)
XLA Modules:
  0.0 189.1 jit_solution(17107376556910669367)
XLA Ops:
  7.2 33.8 %negate_convert_fusion = (bf16[2048,1024]{1,0:T(8,128)(2,1)S(1)}, bf16[2048,1024]{1,0:T(8,128)(2,1)S(1)}) fusion(), kind=kLoop, calls=%fused_computation.14 | loop fusion | flops 35651584 | bytes 8388608 | tf_op jit(solution)/shard_map/convert.1
  41.1 5.1 %fusion.15 = (f32[256]{0:T(256)S(1)}, f32[2048,256]{0,1:T(8,128)}) fusion(bf16[2048,1024]{1,0:T(8,128)(2,1)S(1)} %get-tuple-element.47, bf16[2048,1024]{1,0:T(8,128)(2,1)S(1)} %get-tuple-element.48, bf16[32,8,2048]{2,1,0:T(8,128)(2,1)S(1)} %copy-done), kind=kOutput, calls=%fused_computation.27 | convolution fusion | flops 2165309184 | bytes 11535360 | tf_op jit(solution)/shard_map/dot_general | solution.py:53
  46.3 1.9 %fusion.28 = (f32[32,8,2048]{2,1,0:T(8,128)S(1)}, bf16[32,8,2048]{2,1,0:T(8,128)(2,1)S(1)}) fusion(f32[32]{0:T(128)S(1)} %subtract_convert_fusion, f32[32,8]{1,0:T(8,128)S(1)} %rsqrt.12, f32[2048,256]{0,1:T(8,128)} %get-tuple-element.46), kind=kLoop, calls=%fused_computation.79 | loop fusion | flops 2097152 | bytes 5244032 | tf_op jit(solution)/shard_map/convert_element_type | solution.py:40
  48.7 17.5 %collective-permute-done = bf16[32,8,2048]{2,1,0:T(8,128)(2,1)S(1)} collective-permute-done((bf16[32,8,2048]{2,1,0:T(8,128)(2,1)S(1)}, bf16[32,8,2048]{2,1,0:T(8,128)(2,1)S(1)}, u32[]{:S(2)}, u32[]{:S(2)}) %collective-permute-start) | collective-permute-done | bytes 1048608 | tf_op jit(solution)/shard_map/ppermute | solution.py:13
  66.2 1.0 copy-done.2
  67.2 17.0 %collective-permute-done.1 = bf16[32,8,2048]{2,1,0:T(8,128)(2,1)} collective-permute-done((bf16[32,8,2048]{2,1,0:T(8,128)(2,1)S(1)}, bf16[32,8,2048]{2,1,0:T(8,128)(2,1)}, u32[]{:S(2)}, u32[]{:S(2)}) %collective-permute-start.1) | collective-permute-done | bytes 1048608 | tf_op jit(solution)/shard_map/ppermute | solution.py:13
  84.3 2.8 %gather_fusion = bf16[32,8,2048]{2,1,0:T(8,128)(2,1)} fusion(bf16[32,8,2048]{2,1,0:T(8,128)(2,1)} %copy-done.2, s32[1024]{0:T(1024)S(1)} %pad_clamp_fusion.3), kind=kCustom, calls=%fused_computation.clone | custom fusion | bytes 2097280 | tf_op jit(solution)/shard_map/jit(_take)/gather | solution.py:64
  87.1 2.8 %select_convert_fusion.3 = f32[32,8,2048]{2,1,0:T(8,128)} fusion(bf16[32,8,2048]{2,1,0:T(8,128)(2,1)} %gather_fusion, pred[32]{0:T(512)(128)(4,1)S(1)} %get-tuple-element.39), kind=kLoop, calls=%fused_computation.44 | loop fusion | flops 1048576 | bytes 3145760 | tf_op jit(solution)/shard_map/convert_element_type | solution.py:41
  89.9 2.8 %gather_fusion.1 = bf16[32,8,2048]{2,1,0:T(8,128)(2,1)} fusion(bf16[32,8,2048]{2,1,0:T(8,128)(2,1)} %collective-permute-done.1, s32[1024]{0:T(1024)S(1)} %pad_clamp_fusion.2), kind=kCustom, calls=%fused_computation.1.clone | custom fusion | bytes 2097280 | tf_op jit(solution)/shard_map/jit(_take)/gather | solution.py:64
  92.7 8.7 %collective-permute-done.2 = bf16[32,8,2048]{2,1,0:T(8,128)(2,1)} collective-permute-done((bf16[32,8,2048]{2,1,0:T(8,128)(2,1)}, bf16[32,8,2048]{2,1,0:T(8,128)(2,1)}, u32[]{:S(2)}, u32[]{:S(2)}) %collective-permute-start.2) | collective-permute-done | bytes 1048608 | tf_op jit(solution)/shard_map/ppermute | solution.py:13
  101.5 2.7 %select_convert_fusion.2 = f32[32,8,2048]{2,1,0:T(8,128)} fusion(bf16[32,8,2048]{2,1,0:T(8,128)(2,1)} %gather_fusion.1, pred[32]{0:T(512)(128)(4,1)S(1)} %get-tuple-element.19), kind=kLoop, calls=%fused_computation.43 | loop fusion | flops 1048576 | bytes 3145760 | tf_op jit(solution)/shard_map/convert_element_type | solution.py:41
  104.2 2.9 %gather_fusion.2 = bf16[32,8,2048]{2,1,0:T(8,128)(2,1)} fusion(bf16[32,8,2048]{2,1,0:T(8,128)(2,1)} %collective-permute-done.2, s32[1024]{0:T(1024)S(1)} %pad_clamp_fusion.1), kind=kCustom, calls=%fused_computation.2.clone | custom fusion | bytes 2097280 | tf_op jit(solution)/shard_map/jit(_take)/gather | solution.py:64
  107.1 2.8 %select_convert_fusion.1 = f32[32,8,2048]{2,1,0:T(8,128)} fusion(bf16[32,8,2048]{2,1,0:T(8,128)(2,1)} %gather_fusion.2, pred[32]{0:T(512)(128)(4,1)S(1)} %get-tuple-element.43), kind=kLoop, calls=%fused_computation.42 | loop fusion | flops 1048576 | bytes 3145760 | tf_op jit(solution)/shard_map/convert_element_type | solution.py:41
  109.9 8.8 %collective-permute-done.3 = bf16[32,8,2048]{2,1,0:T(8,128)(2,1)} collective-permute-done((bf16[32,8,2048]{2,1,0:T(8,128)(2,1)}, bf16[32,8,2048]{2,1,0:T(8,128)(2,1)}, u32[]{:S(2)}, u32[]{:S(2)}) %collective-permute-start.3) | collective-permute-done | bytes 1048608 | tf_op jit(solution)/shard_map/ppermute | solution.py:13
  118.7 2.8 %gather_fusion.3 = bf16[32,8,2048]{2,1,0:T(8,128)(2,1)} fusion(bf16[32,8,2048]{2,1,0:T(8,128)(2,1)} %collective-permute-done.3, s32[1024]{0:T(1024)S(1)} %pad_clamp_fusion), kind=kCustom, calls=%fused_computation.3.clone | custom fusion | bytes 2097280 | tf_op jit(solution)/shard_map/jit(_take)/gather | solution.py:64
  121.5 1.6 select_convert_fusion
  123.4 5.4 %add_reduce_fusion.3 = (f32[32,1024]{1,0:T(8,128)S(1)}, f32[32,1024]{1,0:T(8,128)S(1)}, f32[32,1024]{1,0:T(8,128)S(1)}, f32[32,1024]{1,0:T(8,128)S(1)}, f32[32,1...) fusion(f32[32,8,2048]{2,1,0:T(8,128)S(1)} %copy-done.1, ...), kind=kLoop, calls=%fused_computation.52 | loop fusion | flops 8126464 | bytes 11534336 | tf_op jit(solution)/shard_map/reduce_sum | solution.py:44
  129.0 1.1 pad_maximum_fusion
  130.2 4.3 %fusion.24 = (f32[1024,257]{0,1:T(8,128)S(1)}, f32[1024,257]{0,1:T(8,128)S(1)}) fusion(s32[257]{0:T(512)S(1)} %add_select_fusion.2), kind=kLoop, calls=%fused_computation.53 | loop fusion | flops 3947520 | bytes 2106372 | tf_op jit(solution)/shard_map/cos | solution.py:31
  134.5 33.5 %all-reduce.2.cloned.1.call-done = f32[32,4,2048]{2,0,1:T(8,128)} async-done(((f32[32,4,2048]{2,0,1:T(8,128)}), f32[32,4,2048]{2,0,1:T(8,128)}) %all-reduce.2.cloned.1.call-update) | async-done | bytes 1048592 | tf_op jit(solution)/shard_map/psum | solution.py:69
  168.0 4.1 %fusion.16 = f32[32,4,257]{2,0,1:T(8,128)S(1)} fusion(f32[32,4,2048]{2,0,1:T(8,128)} %all-reduce.2.cloned.1.call-done, f32[1024,257]{0,1:T(8,128)S(1)} %get-tuple-element.38, f32[1024,257]{0,1:T(8,128)S(1)} %get-tuple-element.37), kind=kOutput, calls=%fused_computation.31 | convolution fusion | flops 809011328 | bytes 3285504 | tf_op jit(solution)/shard_map/dot_general | solution.py:71
  172.5 3.3 %collective-permute-start.7 = (f32[32,257]{1,0:T(8,128)S(1)}, f32[32,257]{1,0:T(8,128)S(1)}, u32[]{:S(2)}, u32[]{:S(2)}) collective-permute-start(f32[32,257]{1,0:T(8,128)S(1)} %slice_bitcast_fusion.3), channel_id=1, source_target_pairs={{0,24},{2,26},{4,28},{6,30},{8,0},{10,2},{12,4},{14,6},{16,8},{18,... | collective-permute-start | bytes 98696 | tf_op jit(solution)/shard_map/ppermute | solution.py:13
  176.5 1.5 collective-permute-start.5
  178.2 1.4 collective-permute-start.4
  (45 shorter events, 4.9 us)
Async XLA Ops:
  7.2 33.9 %copy-start = (bf16[32,8,2048]{2,1,0:T(8,128)(2,1)S(1)}, bf16[32,8,2048]{2,1,0:T(8,128)(2,1)}, u32[]{:S(2)}) copy-start(bf16[32,8,2048]{2,1,0:T(8,128)(2,1)} %param.5) | copy-start | bytes 3145732
  7.2 33.9 %copy-start.4 = (s32[32]{0:T(128)S(1)}, s32[32]{0:T(128)}, u32[]{:S(2)}) copy-start(s32[32]{0:T(128)} %param.7) | copy-start | bytes 388
  7.2 160.8 %all-reduce.2.cloned.1.call-start = ((), (), s32[]{:S(2)}) async-start(), calls=%async_computation | async-start | bytes 2097152 | tf_op jit(solution)/shard_map/psum | solution.py:69
  46.3 38.0 %copy-start.3 = (s32[4,32]{1,0:T(4,128)S(1)}, s32[4,32]{1,0:T(4,128)}, u32[]{:S(2)}) copy-start(s32[4,32]{1,0:T(4,128)} %param.6) | copy-start | bytes 1540
  48.2 18.0 %collective-permute-start = (bf16[32,8,2048]{2,1,0:T(8,128)(2,1)S(1)}, bf16[32,8,2048]{2,1,0:T(8,128)(2,1)S(1)}, u32[]{:S(2)}, u32[]{:S(2)}) collective-permute-start(bf16[32,8,2048]{2,1,0:T(8,128)(2,1)S(1)} %get-tuple-element.26), channel_id=1, source_target_pairs={{0,2},{2,4},{4,6},{6,8},{8,10},{10,12},{12,14},{14,16},{16,18},{18... | collective-permute-start | bytes 3145736 | tf_op jit(solution)/shard_map/ppermute | solution.py:13
  66.2 1.0 copy-start.2
  67.2 17.0 %collective-permute-start.1 = (bf16[32,8,2048]{2,1,0:T(8,128)(2,1)S(1)}, bf16[32,8,2048]{2,1,0:T(8,128)(2,1)}, u32[]{:S(2)}, u32[]{:S(2)}) collective-permute-start(bf16[32,8,2048]{2,1,0:T(8,128)(2,1)S(1)} %collective-permute-done), channel_id=1, source_target_pairs={{0,2},{2,4},{4,6},{6,8},{8,10},{10,12},{12,14},{14,16},{16,18},{18... | collective-permute-start | bytes 3145736 | tf_op jit(solution)/shard_map/ppermute | solution.py:13
  84.2 17.2 %collective-permute-start.2 = (bf16[32,8,2048]{2,1,0:T(8,128)(2,1)}, bf16[32,8,2048]{2,1,0:T(8,128)(2,1)}, u32[]{:S(2)}, u32[]{:S(2)}) collective-permute-start(bf16[32,8,2048]{2,1,0:T(8,128)(2,1)} %collective-permute-done.1), channel_id=1, source_target_pairs={{0,2},{2,4},{4,6},{6,8},{8,10},{10,12},{12,14},{14,16},{16,18},{18... | collective-permute-start | bytes 3145736 | tf_op jit(solution)/shard_map/ppermute | solution.py:13
  101.5 17.2 %collective-permute-start.3 = (bf16[32,8,2048]{2,1,0:T(8,128)(2,1)}, bf16[32,8,2048]{2,1,0:T(8,128)(2,1)}, u32[]{:S(2)}, u32[]{:S(2)}) collective-permute-start(bf16[32,8,2048]{2,1,0:T(8,128)(2,1)} %collective-permute-done.2), channel_id=1, source_target_pairs={{0,2},{2,4},{4,6},{6,8},{8,10},{10,12},{12,14},{14,16},{16,18},{18... | collective-permute-start | bytes 3145736 | tf_op jit(solution)/shard_map/ppermute | solution.py:13
  121.5 1.9 %copy-start.1 = (f32[32,8,2048]{2,1,0:T(8,128)S(1)}, f32[32,8,2048]{2,1,0:T(8,128)}, u32[]{:S(2)}) copy-start(f32[32,8,2048]{2,1,0:T(8,128)} %select_convert_fusion.3) | copy-start | bytes 6291460
  172.5 8.0 %collective-permute-start.7 = (f32[32,257]{1,0:T(8,128)S(1)}, f32[32,257]{1,0:T(8,128)S(1)}, u32[]{:S(2)}, u32[]{:S(2)}) collective-permute-start(f32[32,257]{1,0:T(8,128)S(1)} %slice_bitcast_fusion.3), channel_id=1, source_target_pairs={{0,24},{2,26},{4,28},{6,30},{8,0},{10,2},{12,4},{14,6},{16,8},{18,... | collective-permute-start | bytes 98696 | tf_op jit(solution)/shard_map/ppermute | solution.py:13
  176.1 4.3 %collective-permute-start.6 = (f32[32,257]{1,0:T(8,128)S(1)}, f32[32,257]{1,0:T(8,128)S(1)}, u32[]{:S(2)}, u32[]{:S(2)}) collective-permute-start(f32[32,257]{1,0:T(8,128)S(1)} %slice_bitcast_fusion.2), channel_id=1, source_target_pairs={{0,26},{2,28},{4,30},{6,0},{8,2},{10,4},{12,6},{14,8},{16,10},{18,... | collective-permute-start | bytes 98696 | tf_op jit(solution)/shard_map/ppermute | solution.py:13
  176.5 4.1 %collective-permute-start.5 = (f32[32,257]{1,0:T(8,128)S(1)}, f32[32,257]{1,0:T(8,128)S(1)}, u32[]{:S(2)}, u32[]{:S(2)}) collective-permute-start(f32[32,257]{1,0:T(8,128)S(1)} %slice_bitcast_fusion.1), channel_id=1, source_target_pairs={{0,28},{2,30},{4,0},{6,2},{8,4},{10,6},{12,8},{14,10},{16,12},{18,... | collective-permute-start | bytes 98696 | tf_op jit(solution)/shard_map/ppermute | solution.py:13
  178.2 3.2 %collective-permute-start.4 = (f32[32,257]{1,0:T(8,128)S(1)}, f32[32,257]{1,0:T(8,128)S(1)}, u32[]{:S(2)}, u32[]{:S(2)}) collective-permute-start(f32[32,257]{1,0:T(8,128)S(1)} %slice_bitcast_fusion), channel_id=1, source_target_pairs={{0,30},{2,0},{4,2},{6,4},{8,6},{10,8},{12,10},{14,12},{16,14},{18,... | collective-permute-start | bytes 98696 | tf_op jit(solution)/shard_map/ppermute | solution.py:13
Sparse Core Ops, SparseCore 0:
  130.3 37.7 all-reduce.1
where the time goes:
time: 190 us; the launch traced here: 189 us
  waiting for transfers between devices  86.6 us (46%)
  other arithmetic  56.7 us (30%)
  local copies, waits for them, and re-layouts  15.6 us (8%)
  between operations  14.2 us (7%)
  matrix products  9.18 us (5%)
  starting transfers between devices  6.8 us (4%)
    ppermute x8, waiting for transfers between devices, shifted(): lax.ppermute(x, axis, [(i, (i + by) % length) for i in range(length)])  53 us
    another operation x1, other arithmetic  33.8 us
    psum x1, waiting for transfers between devices, on_device(): stacked = lax.psum(cross, 'rep')  33.5 us
    gather x4, local copies, waits for them, and re-layouts, on_device(): partner = jnp.take(moving, offsets[stop - 1], axis=0)  11.4 us
    convert_element_type x4, other arithmetic, cross_spectrum(): second = partner.astype(jnp.float32)  9.85 us
    ppermute x8, starting transfers between devices, shifted(): lax.ppermute(x, axis, [(i, (i + by) % length) for i in range(length)])  6.76 us
    reduce_sum x1, other arithmetic, cross_spectrum(): real_sum = jnp.sum(real_a * real_b + imag_a * imag_b, axis=1)  5.42 us
    dot_general x1, matrix products, on_device(): jnp.dot(samples.reshape(channels * segments, length), forward_table(lengt...  5.05 us
  transfers between devices with their start and end apart: 9, of which 7 were waited for; matrix products, arithmetic and copies ran while one was open for 12% of the time, Pallas kernels for 0%

commit v1 on v0

--- a/solution.py
+++ b/solution.py
@@ -2,6 +2,8 @@
 
 import jax
 import jax.numpy as jnp
+import ml_dtypes
+import numpy as np
 from jax import lax
 from jax.sharding import PartitionSpec as P
 
@@ -14,21 +16,16 @@
 
 
 def forward_table(length):
-    half_len = length // 2
-    sample_idx = lax.iota(jnp.int32, length)
-    bin_idx = lax.iota(jnp.int32, half_len)
-    phase = sample_idx[:, None] * bin_idx[None, :] % length
-    angle = phase.astype(jnp.float32) * (2.0 * math.pi / length)
-    return jnp.concatenate([jnp.cos(angle), -jnp.sin(angle)], axis=1).astype(jnp.bfloat16)
+    phase = np.arange(length)[:, None] * np.arange(length // 2)[None, :] % length
+    angle = phase * (2.0 * math.pi / length)
+    return np.concatenate([np.cos(angle), -np.sin(angle)], axis=1).astype(ml_dtypes.bfloat16)
 
 
 def inverse_table(length, lag_half):
-    half_len = length // 2
-    bin_idx = lax.iota(jnp.int32, half_len)
-    lag_idx = lax.iota(jnp.int32, 2 * lag_half + 1) - lag_half
-    phase = bin_idx[:, None] * (lag_idx[None, :] % length) % length
-    angle = phase.astype(jnp.float32) * (2.0 * math.pi / length)
-    return jnp.concatenate([jnp.cos(angle), -jnp.sin(angle)], axis=0)
+    lag_idx = np.arange(2 * lag_half + 1) - lag_half
+    phase = np.arange(length // 2)[:, None] * (lag_idx[None, :] % length) % length
+    angle = phase * (2.0 * math.pi / length)
+    return np.concatenate([np.cos(angle), -np.sin(angle)], axis=0).astype(np.float32)
 
 
 def whiten(spectrum, keep, half_len):
@@ -52,7 +49,7 @@
     stops = offsets.shape[0]
     spectrum = jnp.dot(
         samples.reshape(channels * segments, length),
-        forward_table(length),
+        jnp.asarray(forward_table(length)),
         preferred_element_type=jnp.float32,
     ).reshape(channels, segments, length)
     keep = (1 - bad_mask).astype(jnp.float32)
@@ -65,17 +62,13 @@
         pieces.append(cross_spectrum(white, partner, half_len))
     cross = jnp.stack(pieces, axis=1)
     scale = 1.0 / math.sqrt(segments * lax.axis_size("rep") * half_len)
-    back_table = inverse_table(length, LAGS)
-    stacked = lax.psum(cross, "rep")
-    correlations = (
-        jnp.dot(
-            stacked.reshape(channels * stops, length),
-            back_table,
-            precision=lax.Precision.HIGHEST,
-            preferred_element_type=jnp.float32,
-        ).reshape(channels, stops, -1)
-        * scale
-    )
+    partial = jnp.dot(
+        cross.reshape(channels * stops, length),
+        jnp.asarray(inverse_table(length, LAGS)),
+        precision=lax.Precision.HIGHEST,
+        preferred_element_type=jnp.float32,
+    ).reshape(channels, stops, -1)
+    correlations = lax.psum(partial, "rep") * scale
     mirrored = []
     for stop in range(1, stops + 1):
         flipped = correlations[:, stop - 1, ::-1]

time: 190 us -> 148 us (0.78)
  other arithmetic: 56.7 us -> 13.8 us
  local copies, waits for them, and re-layouts: 15.6 us -> 25.8 us
  waiting for transfers between devices: 86.6 us -> 77 us
    another operation x1 -> x0, other arithmetic: 33.8 us -> none
    ppermute x0 -> x4, local copies, waits for them, and re-layouts: none -> 10 us  [shifted(): lax.ppermute(x, axis, [(i, (i + by) % length) for i in range(length)])]
    psum x1, waiting for transfers between devices: 33.5 us -> 24.1 us  [on_device(): correlations = lax.psum(partial, 'rep') * scale]
    cos x1 -> x0, other arithmetic: 4.33 us -> none  [inverse_table(): return jnp.concatenate([jnp.cos(angle), -jnp.sin(angle)], axis=0)]
    reduce_sum x1, other arithmetic: 5.42 us -> 1.39 us  [cross_spectrum(): real_sum = jnp.sum(real_a * real_b + imag_a * imag_b, axis=1)]
    unnamed x16 -> x18, local copies, waits for them, and re-layouts: 3.86 us -> 4.12 us
    convert_element_type x4 -> x2, other arithmetic: 9.85 us -> 10 us  [cross_spectrum(): second = partner.astype(jnp.float32)]
  transfers between devices with their start and end apart: 9 -> 9, of which waited for: 7 -> 6; matrix products, arithmetic and copies ran while one was open for 12% -> 15% of each run, Pallas kernels for 0% -> 0%
where the time goes in v1:
time: 148 us; the launch traced here: 147 us
  waiting for transfers between devices  77 us (52%)
  local copies, waits for them, and re-layouts  25.8 us (17%)
  between operations  14.2 us (10%)
  other arithmetic  13.8 us (9%)
  matrix products  9.51 us (6%)
  starting transfers between devices  6.78 us (5%)
    ppermute x8, waiting for transfers between devices, shifted(): lax.ppermute(x, axis, [(i, (i + by) % length) for i in range(length)])  52.9 us
    psum x1, waiting for transfers between devices, on_device(): correlations = lax.psum(partial, 'rep') * scale  24.1 us
    gather x4, local copies, waits for them, and re-layouts, on_device(): partner = jnp.take(moving, offsets[stop - 1], axis=0)  11.3 us
    ppermute x4, local copies, waits for them, and re-layouts, shifted(): lax.ppermute(x, axis, [(i, (i + by) % length) for i in range(length)])  10 us
    convert_element_type x2, other arithmetic, cross_spectrum(): second = partner.astype(jnp.float32)  10 us
    ppermute x8, starting transfers between devices, shifted(): lax.ppermute(x, axis, [(i, (i + by) % length) for i in range(length)])  6.75 us
    dot_general x1, matrix products, on_device(): jnp.dot(samples.reshape(channels * segments, length), jnp.asarray(forward...  5.93 us
    unnamed x18, local copies, waits for them, and re-layouts  4.12 us
  transfers between devices with their start and end apart: 9, of which 6 were waited for; matrix products, arithmetic and copies ran while one was open for 15% of the time, Pallas kernels for 0%

profile of v1, /device:TPU:0, one launch (start us, length us, event | category | flops | bytes accessed | tf_op | source)
XLA Modules:
  0.0 147.1 jit_solution(1561126682661585277)
XLA Ops:
  8.4 5.9 %multiply_reduce_fusion = (f32[32,8]{0,1:T(8,128)S(1)}, f32[2048,32,8]{0,1,2:T(8,128)S(1)}) fusion(bf16[2048,2048,1]{1,0,2:T(8,128)(2,1)} %constant.27, bf16[32,8,2048]{2,1,0:T(8,128)(2,1)S(1)} %copy-done), kind=kOutput, calls=%fused_computation.5 | convolution fusion | flops 2148531968 | bytes 11535360 | tf_op jit(solution)/shard_map/dot_general | solution.py:50
  15.4 17.5 %collective-permute-done = bf16[32,8,2048]{2,0,1:T(8,128)(2,1)S(1)} collective-permute-done((bf16[32,8,2048]{2,0,1:T(8,128)(2,1)S(1)}, bf16[32,8,2048]{2,0,1:T(8,128)(2,1)S(1)}, u32[]{:S(2)}, u32[]{:S(2)}) %collective-permute-start) | collective-permute-done | bytes 1048608 | tf_op jit(solution)/shard_map/ppermute | solution.py:15
  32.9 16.9 %collective-permute-done.1 = bf16[32,8,2048]{2,0,1:T(8,128)(2,1)S(1)} collective-permute-done((bf16[32,8,2048]{2,0,1:T(8,128)(2,1)S(1)}, bf16[32,8,2048]{2,0,1:T(8,128)(2,1)S(1)}, u32[]{:S(2)}, u32[]{:S(2)}) %collective-permute-start.1) | collective-permute-done | bytes 1048608 | tf_op jit(solution)/shard_map/ppermute | solution.py:15
  49.8 1.0 copy-done.4
  50.8 17.0 %collective-permute-done.2 = bf16[32,8,2048]{2,0,1:T(8,128)(2,1)} collective-permute-done((bf16[32,8,2048]{2,0,1:T(8,128)(2,1)S(1)}, bf16[32,8,2048]{2,0,1:T(8,128)(2,1)}, u32[]{:S(2)}, u32[]{:S(2)}) %collective-permute-start.2) | collective-permute-done | bytes 1048608 | tf_op jit(solution)/shard_map/ppermute | solution.py:15
  67.9 1.6 %copy.11 = bf16[32,8,2048]{2,1,0:T(8,128)(2,1)} copy(bf16[32,8,2048]{2,0,1:T(8,128)(2,1)S(1)} %collective-permute-done) | data formatting | bytes 2097152 | tf_op jit(solution)/shard_map/ppermute | solution.py:15
  69.5 2.8 %gather_fusion = bf16[32,8,2048]{2,1,0:T(8,128)(2,1)} fusion(bf16[32,8,2048]{2,1,0:T(8,128)(2,1)} %copy.11, s32[1024]{0:T(1024)S(1)} %pad_clamp_fusion.3), kind=kCustom, calls=%fused_computation.clone | custom fusion | bytes 2097280 | tf_op jit(solution)/shard_map/jit(_take)/gather | solution.py:61
  72.4 2.8 %copy.13 = bf16[32,8,2048]{2,1,0:T(8,128)(2,1)} copy(bf16[32,8,2048]{2,0,1:T(8,128)(2,1)} %copy-done.4) | data formatting | bytes 2097152 | tf_op jit(solution)/shard_map/ppermute | solution.py:15
  75.2 2.8 %gather_fusion.1 = bf16[32,8,2048]{2,1,0:T(8,128)(2,1)} fusion(bf16[32,8,2048]{2,1,0:T(8,128)(2,1)} %copy.13, s32[1024]{0:T(1024)S(1)} %pad_clamp_fusion.2), kind=kCustom, calls=%fused_computation.1.clone | custom fusion | bytes 2097280 | tf_op jit(solution)/shard_map/jit(_take)/gather | solution.py:61
  78.0 5.9 %fusion.11 = (f32[32,8,2048]{2,0,1:T(8,128)}, f32[32,8,2048]{2,0,1:T(8,128)}) fusion(bf16[32,8,2048]{2,1,0:T(8,128)(2,1)} %gather_fusion.1, pred[32]{0:T(512)(128)(4,1)S(1)} %get-tuple-element.19, bf16[32,8,2048]{2,1,0:T(8,128)(2,1)} %gather_fusion, pred[32]{0:T(512)(128)(4,1)S(1)} %get-tuple-element.37), kind=kLoop, calls=%fused_computation.20 | loop fusion | flops 2097152 | bytes 6291520 | tf_op jit(solution)/shard_map/convert_element_type | solution.py:38
  83.9 2.8 %copy.15 = bf16[32,8,2048]{2,1,0:T(8,128)(2,1)} copy(bf16[32,8,2048]{2,0,1:T(8,128)(2,1)} %collective-permute-done.2) | data formatting | bytes 2097152 | tf_op jit(solution)/shard_map/ppermute | solution.py:15
  86.7 2.8 %gather_fusion.2 = bf16[32,8,2048]{2,1,0:T(8,128)(2,1)} fusion(bf16[32,8,2048]{2,1,0:T(8,128)(2,1)} %copy.15, s32[1024]{0:T(1024)S(1)} %pad_clamp_fusion.1), kind=kCustom, calls=%fused_computation.2.clone | custom fusion | bytes 2097280 | tf_op jit(solution)/shard_map/jit(_take)/gather | solution.py:61
  89.5 2.8 %copy.17 = bf16[32,8,2048]{2,1,0:T(8,128)(2,1)} copy(bf16[32,8,2048]{2,0,1:T(8,128)(2,1)} %collective-permute-done.3) | data formatting | bytes 2097152 | tf_op jit(solution)/shard_map/ppermute | solution.py:15
  92.3 2.8 %gather_fusion.3 = bf16[32,8,2048]{2,1,0:T(8,128)(2,1)} fusion(bf16[32,8,2048]{2,1,0:T(8,128)(2,1)} %copy.17, s32[1024]{0:T(1024)S(1)} %pad_clamp_fusion), kind=kCustom, calls=%fused_computation.3.clone | custom fusion | bytes 2097280 | tf_op jit(solution)/shard_map/jit(_take)/gather | solution.py:61
  95.2 4.1 %fusion.9 = (f32[32,8,2048]{2,0,1:T(8,128)S(1)}, f32[32,8,2048]{2,0,1:T(8,128)S(1)}) fusion(bf16[32,8,2048]{2,1,0:T(8,128)(2,1)} %gather_fusion.3, pred[32]{0:T(512)(128)(4,1)S(1)} %get-tuple-element.39, bf16[32,8,2048]{2,1,0:T(8,128)(2,1)} %gather_fusion.2, pred[32]{0:T(512)(128)(4,1)S(1)} %get-tuple-element.41), kind=kLoop, calls=%fused_computation.16 | loop fusion | flops 2097152 | bytes 6291520 | tf_op jit(solution)/shard_map/convert_element_type | solution.py:38
  99.3 1.4 add_reduce_fusion.3
  100.9 3.6 %fusion.1 = f32[32,4,257]{2,0,1:T(8,128)} fusion(f32[2048,257,1]{0,1,2:T(8,128)S(1)} %copy-done.3, f32[32,1,2048]{2,0,1:T(8,128)S(1)} %maximum_bitcast_fusion.3, f32[32,1,2048]{2,0,1:T(8,128)S(1)} %maximum_bitcast_fusion.2, f32[32,1,2048]{2,0,1:T(8,128)S(1)} %maximum_bitcast_fusion.1, f32[32,1,2048]{2,0,1:T(8,128)S(1)} %maximum_bitcast_fusion), kind=kOutput, calls=%fused_computation.7 | convolution fusion | flops 809238528 | bytes 3285504 | tf_op jit(solution)/shard_map/dot_general | solution.py:65
  104.5 24.1 %all-reduce.2.cloned.1.call-done = f32[32,4,257]{2,0,1:T(8,128)} async-done(((f32[32,4,257]{2,0,1:T(8,128)}), f32[32,4,257]{2,0,1:T(8,128)}) %all-reduce.2.cloned.1.call-update) | async-done | bytes 131600 | tf_op jit(solution)/shard_map/psum | solution.py:71
  128.6 0.9 broadcast_multiply_fusion
  130.8 4.3 %collective-permute-start.5 = (f32[32,257]{1,0:T(8,128)S(1)}, f32[32,257]{1,0:T(8,128)S(1)}, u32[]{:S(2)}, u32[]{:S(2)}) collective-permute-start(f32[32,257]{1,0:T(8,128)S(1)} %slice_bitcast_fusion.1), channel_id=1, source_target_pairs={{0,28},{2,30},{4,0},{6,2},{8,4},{10,6},{12,8},{14,10},{16,12},{18,... | collective-permute-start | bytes 98696 | tf_op jit(solution)/shard_map/ppermute | solution.py:15
  135.6 1.4 collective-permute-start.4
  137.1 0.8 copy.19
  138.6 0.8 collective-permute-done.7
  139.4 0.8 copy.20
  (45 shorter events, 5.1 us)
Async XLA Ops:
  7.2 1.2 copy-start
  7.2 121.4 %all-reduce.2.cloned.1.call-start = ((), (), s32[]{:S(2)}) async-start(), calls=%async_computation | async-start | bytes 393216 | tf_op jit(solution)/shard_map/psum | solution.py:71
  14.4 36.5 %copy-start.5 = (s32[4,32]{1,0:T(4,128)S(1)}, s32[4,32]{1,0:T(4,128)}, u32[]{:S(2)}) copy-start(s32[4,32]{1,0:T(4,128)} %param.8) | copy-start | bytes 1540
  14.9 18.0 %collective-permute-start = (bf16[32,8,2048]{2,0,1:T(8,128)(2,1)S(1)}, bf16[32,8,2048]{2,0,1:T(8,128)(2,1)S(1)}, u32[]{:S(2)}, u32[]{:S(2)}) collective-permute-start(bf16[32,8,2048]{2,0,1:T(8,128)(2,1)S(1)} %get-tuple-element.26), channel_id=1, source_target_pairs={{0,2},{2,4},{4,6},{6,8},{8,10},{10,12},{12,14},{14,16},{16,18},{18... | collective-permute-start | bytes 3145736 | tf_op jit(solution)/shard_map/ppermute | solution.py:15
  32.9 16.9 %collective-permute-start.1 = (bf16[32,8,2048]{2,0,1:T(8,128)(2,1)S(1)}, bf16[32,8,2048]{2,0,1:T(8,128)(2,1)S(1)}, u32[]{:S(2)}, u32[]{:S(2)}) collective-permute-start(bf16[32,8,2048]{2,0,1:T(8,128)(2,1)S(1)} %collective-permute-done), channel_id=1, source_target_pairs={{0,2},{2,4},{4,6},{6,8},{8,10},{10,12},{12,14},{14,16},{16,18},{18... | collective-permute-start | bytes 3145736 | tf_op jit(solution)/shard_map/ppermute | solution.py:15
  49.8 1.0 copy-start.4
  50.8 17.0 %collective-permute-start.2 = (bf16[32,8,2048]{2,0,1:T(8,128)(2,1)S(1)}, bf16[32,8,2048]{2,0,1:T(8,128)(2,1)}, u32[]{:S(2)}, u32[]{:S(2)}) collective-permute-start(bf16[32,8,2048]{2,0,1:T(8,128)(2,1)S(1)} %collective-permute-done.1), channel_id=1, source_target_pairs={{0,2},{2,4},{4,6},{6,8},{8,10},{10,12},{12,14},{14,16},{16,18},{18... | collective-permute-start | bytes 3145736 | tf_op jit(solution)/shard_map/ppermute | solution.py:15
  67.8 21.7 %collective-permute-start.3 = (bf16[32,8,2048]{2,0,1:T(8,128)(2,1)}, bf16[32,8,2048]{2,0,1:T(8,128)(2,1)}, u32[]{:S(2)}, u32[]{:S(2)}) collective-permute-start(bf16[32,8,2048]{2,0,1:T(8,128)(2,1)} %collective-permute-done.2), channel_id=1, source_target_pairs={{0,2},{2,4},{4,6},{6,8},{8,10},{10,12},{12,14},{14,16},{16,18},{18... | collective-permute-start | bytes 3145736 | tf_op jit(solution)/shard_map/ppermute | solution.py:15
  95.2 4.1 %copy-start.1 = (f32[32,8,2048]{2,0,1:T(8,128)S(1)}, f32[32,8,2048]{2,0,1:T(8,128)}, u32[]{:S(2)}) copy-start(f32[32,8,2048]{2,0,1:T(8,128)} %get-tuple-element.47) | copy-start | bytes 6291460
  95.2 4.1 %copy-start.2 = (f32[32,8,2048]{2,0,1:T(8,128)S(1)}, f32[32,8,2048]{2,0,1:T(8,128)}, u32[]{:S(2)}) copy-start(f32[32,8,2048]{2,0,1:T(8,128)} %get-tuple-element.48) | copy-start | bytes 6291460
  99.3 1.6 %copy-start.3 = (f32[2048,257,1]{0,1,2:T(8,128)S(1)}, f32[2048,257,1]{0,1,2:T(8,128)}, u32[]{:S(2)}) copy-start(f32[2048,257,1]{0,1,2:T(8,128)} %constant.28) | copy-start | bytes 6316036
  130.8 7.0 %collective-permute-start.5 = (f32[32,257]{1,0:T(8,128)S(1)}, f32[32,257]{1,0:T(8,128)S(1)}, u32[]{:S(2)}, u32[]{:S(2)}) collective-permute-start(f32[32,257]{1,0:T(8,128)S(1)} %slice_bitcast_fusion.1), channel_id=1, source_target_pairs={{0,28},{2,30},{4,0},{6,2},{8,4},{10,6},{12,8},{14,10},{16,12},{18,... | collective-permute-start | bytes 98696 | tf_op jit(solution)/shard_map/ppermute | solution.py:15
  135.1 3.5 %collective-permute-start.6 = (f32[32,257]{1,0:T(8,128)S(1)}, f32[32,257]{1,0:T(8,128)S(1)}, u32[]{:S(2)}, u32[]{:S(2)}) collective-permute-start(f32[32,257]{1,0:T(8,128)S(1)} %slice_bitcast_fusion.2), channel_id=1, source_target_pairs={{0,26},{2,28},{4,30},{6,0},{8,2},{10,4},{12,6},{14,8},{16,10},{18,... | collective-permute-start | bytes 98696 | tf_op jit(solution)/shard_map/ppermute | solution.py:15
  135.1 4.3 %collective-permute-start.7 = (f32[32,257]{1,0:T(8,128)S(1)}, f32[32,257]{1,0:T(8,128)S(1)}, u32[]{:S(2)}, u32[]{:S(2)}) collective-permute-start(f32[32,257]{1,0:T(8,128)S(1)} %slice_bitcast_fusion.3), channel_id=1, source_target_pairs={{0,24},{2,26},{4,28},{6,30},{8,0},{10,2},{12,4},{14,6},{16,8},{18,... | collective-permute-start | bytes 98696 | tf_op jit(solution)/shard_map/ppermute | solution.py:15
  135.6 3.8 %collective-permute-start.4 = (f32[32,257]{1,0:T(8,128)S(1)}, f32[32,257]{1,0:T(8,128)S(1)}, u32[]{:S(2)}, u32[]{:S(2)}) collective-permute-start(f32[32,257]{1,0:T(8,128)S(1)} %slice_bitcast_fusion), channel_id=1, source_target_pairs={{0,30},{2,0},{4,2},{6,4},{8,6},{10,8},{12,10},{14,12},{16,14},{18,... | collective-permute-start | bytes 98696 | tf_op jit(solution)/shard_map/ppermute | solution.py:15
Sparse Core Ops, SparseCore 0:
  104.7 23.8 all-reduce.1

commit v2 on v1

v2 whole, which is shorter than its diff:
```python
import functools
import math

import jax
import jax.numpy as jnp
import ml_dtypes
import numpy as np
from jax import lax
from jax.experimental import pallas as pl
from jax.experimental.pallas import tpu as pltpu
from jax.sharding import PartitionSpec as P

LAGS = 128
LANES = 128
MESH = pl.DeviceIdType.MESH
F32 = jnp.float32
BF16 = jnp.bfloat16


def forward_table(length, bins):
    phase = np.arange(length)[:, None] * np.arange(length // 2)[None, :] % length
    angle = phase * (2.0 * math.pi / length)
    real = np.cos(angle).reshape(length, -1, bins)
    imag = -np.sin(angle).reshape(length, -1, bins)
    both = np.concatenate([real, imag], axis=2).transpose(1, 0, 2)
    return np.ascontiguousarray(both).astype(ml_dtypes.bfloat16)


def inverse_table(length, lag_half, bins, padded):
    width = 2 * lag_half + 1
    lag_idx = np.arange(width) - lag_half
    phase = np.arange(length // 2)[:, None] * (lag_idx[None, :] % length) % length
    angle = phase * (2.0 * math.pi / length)
    whole = np.zeros((2, length // 2, padded), np.float32)
    whole[0, :, :width] = np.cos(angle)
    whole[1, :, :width] = np.sin(angle)
    high = whole.astype(ml_dtypes.bfloat16)
    low = (whole - high.astype(np.float32)).astype(ml_dtypes.bfloat16)
    both = np.stack([high, low], axis=1).reshape(2, 2, -1, bins, padded)
    return np.ascontiguousarray(both.transpose(2, 0, 1, 3, 4))


def kernel(
    scale,
    groups,
    samples, table, back, offsets, bad,
    corr, mirr,
    table_v, back_v, spec, norm, own, part, peer, even, odd_, flip,
    table_sem, back_sem, send_sem, recv_sem, rep_send, rep_recv, mir_send, mir_recv,
    *far_flat,
):
    stops, channels, padded = corr.shape
    rows = samples.shape[0]
    segs = rows // channels
    bins = own.shape[-1]
    far = [far_flat[d * groups:(d + 1) * groups] for d in range(stops)]
    blk, rep = lax.axis_index("blk"), lax.axis_index("rep")
    n = lax.axis_size("blk")
    core = lax.rem(blk, 2)
    odd = lax.rem(blk // 2, 2)
    up = lax.rem(blk + 4, n)
    beside = blk + 2 - 4 * odd
    sibling = blk + 1 - 2 * core
    other = 1 - rep

    def load(j):
        return pltpu.make_async_copy(table.at[j], table_v.at[j], table_sem.at[j])

    for j in range(groups):
        load(j).start()
    back_load = pltpu.make_async_copy(back, back_v, back_sem)
    back_load.start()

    barrier = pltpu.get_barrier_semaphore()
    for by in range(1, stops + 1):
        for who in (lax.rem(blk + by, n), lax.rem(blk + n - by, n)):
            pl.semaphore_signal(barrier, inc=1, device_id=(who, rep), device_id_type=MESH)
    pl.semaphore_signal(barrier, inc=1, device_id=(blk, other), device_id_type=MESH)
    pl.semaphore_wait(barrier, 2 * stops + 1)

    def send(src, stop, k, lane, who):
        return pltpu.make_async_remote_copy(
            src_ref=src,
            dst_ref=far[stop - 1][k],
            send_sem=send_sem.at[lane, k],
            recv_sem=recv_sem.at[stop - 1, k],
            device_id=(who, rep),
            device_id_type=MESH,
        )

    def arrived(stop, k):
        send(own.at[k], stop, k, 0, up).wait_recv()

    norm[...] = jnp.zeros_like(norm)

    @pl.loop(0, groups)
    def _(j):
        load(j).wait()
        got = jnp.dot(samples[...], table_v[j], preferred_element_type=F32)
        spec[j] = got
        norm[...] += got[:, :bins] * got[:, :bins] + got[:, bins:] * got[:, bins:]

    power = jnp.sum(norm[...], axis=1, keepdims=True) / (groups * bins)
    norm[...] = jnp.broadcast_to(lax.rsqrt(power + 1e-06), norm.shape)
    for c in range(channels):
        norm[c * segs:(c + 1) * segs, :] *= (1 - bad[c]).astype(F32)

    for k in range(groups):
        real = (spec[k, :, :bins] * norm[...]).reshape(channels, segs, bins)
        imag = (spec[k, :, bins:] * norm[...]).reshape(channels, segs, bins)
        own[k] = jnp.concatenate([real, imag], axis=1).astype(BF16)
        send(own.at[k], 4, k, 0, up).start()

        @pl.when(odd == 0)
        def _():
            send(own.at[k], 2, k, 1, beside).start()

        @pl.when(core == 0)
        def _():
            send(own.at[k], 1, k, 2, sibling).start()

    def exchange(k):
        return pltpu.make_async_remote_copy(
            src_ref=part.at[k],
            dst_ref=peer.at[k],
            send_sem=rep_send.at[k],
            recv_sem=rep_recv.at[k],
            device_id=(blk, other),
            device_id_type=MESH,
        )

    even[...] = jnp.zeros_like(even)
    odd_[...] = jnp.zeros_like(odd_)

    def finish(k):
        exchange(k).wait_recv()
        for side, total in ((0, even), (1, odd_)):
            cross = part[k, side] + peer[k, side]
            high = cross.astype(BF16)
            low = (cross - high.astype(F32)).astype(BF16)
            total[...] += (
                jnp.dot(high, back_v[k, side, 0], preferred_element_type=F32)
                + jnp.dot(low, back_v[k, side, 0], preferred_element_type=F32)
                + jnp.dot(high, back_v[k, side, 1], preferred_element_type=F32)
            )

    back_load.wait()
    for k in range(groups):
        arrived(4, k)

        @pl.when(odd == 1)
        def _():
            send(far[3][k], 2, k, 1, beside).start()

        @pl.when(core == 1)
        def _():
            send(far[3][k], 3, k, 3, sibling).start()

        arrived(2, k)

        @pl.when(core == 1)
        def _():
            send(far[1][k], 1, k, 2, sibling).start()

        @pl.when(core == 0)
        def _():
            send(far[1][k], 3, k, 3, sibling).start()

        arrived(3, k)
        arrived(1, k)

        @pl.loop(0, channels // 4)
        def _(quad):
            for u in range(4):
                g = quad * 4 + u
                mine = own[k, g].astype(F32)
                real_a, imag_a = mine[:segs], mine[segs:]
                for d in range(stops):
                    theirs = far[d][k][offsets[d, g]].astype(F32)
                    real_b, imag_b = theirs[:segs], theirs[segs:]
                    row = pl.ds(d * channels + g, 1)
                    part[k, 0, row, :] = jnp.sum(real_a * real_b + imag_a * imag_b, axis=0, keepdims=True)
                    part[k, 1, row, :] = jnp.sum(imag_a * real_b - real_a * imag_b, axis=0, keepdims=True)

        exchange(k).start()
        if k >= 1:
            finish(k - 1)
    finish(groups - 1)

    corr[...] = ((even[...] - odd_[...]) * scale).reshape(corr.shape)
    flip[...] = ((even[...] + odd_[...]) * scale).reshape(flip.shape)
    back_home = [
        pltpu.make_async_remote_copy(
            src_ref=flip.at[d],
            dst_ref=mirr.at[d],
            send_sem=mir_send.at[d],
            recv_sem=mir_recv.at[d],
            device_id=(lax.rem(blk + n - d - 1, n), rep),
            device_id_type=MESH,
        )
        for d in range(stops)
    ]
    for copy in back_home:
        copy.start()
    for k in range(groups):
        for lane in range(4):
            send(own.at[k], 4, k, lane, up).wait_send()
        exchange(k).wait_send()
    for copy in back_home:
        copy.wait()


def on_device(samples, offsets, bad_mask):
    channels, segs, length = samples.shape
    stops = offsets.shape[0]
    rows = channels * segs
    bins = LANES
    groups = length // 2 // bins
    width = 2 * LAGS + 1
    padded = -(-width // LANES) * LANES
    scale = 1.0 / math.sqrt(segs * lax.axis_size("rep") * (length // 2))
    vmem = pl.BlockSpec(memory_space=pltpu.VMEM)
    smem = pl.BlockSpec(memory_space=pltpu.SMEM)
    hbm = pl.BlockSpec(memory_space=pl.ANY)
    out = jax.ShapeDtypeStruct((stops, channels, padded), F32)
    dma = pltpu.SemaphoreType.DMA
    corr, mirr = pl.pallas_call(
        functools.partial(kernel, scale, groups),
        out_shape=(out, out),
        in_specs=[vmem, hbm, hbm, smem, smem],
        out_specs=(vmem, vmem),
        scratch_shapes=[
            pltpu.VMEM((groups, length, 2 * bins), BF16),
            pltpu.VMEM((groups, 2, 2, bins, padded), BF16),
            pltpu.VMEM((groups, rows, 2 * bins), F32),
            pltpu.VMEM((rows, bins), F32),
            pltpu.VMEM((groups, channels, 2 * segs, bins), BF16),
            pltpu.VMEM((groups, 2, stops * channels, bins), F32),
            pltpu.VMEM((groups, 2, stops * channels, bins), F32),
            pltpu.VMEM((stops * channels, padded), F32),
            pltpu.VMEM((stops * channels, padded), F32),
            pltpu.VMEM((stops, channels, padded), F32),
            dma((groups,)), dma,
            dma((4, groups)), dma((stops, groups)),
            dma((groups,)), dma((groups,)),
            dma((stops,)), dma((stops,)),
        ] + [pltpu.VMEM((channels, 2 * segs, bins), BF16)] * (stops * groups),
        compiler_params=pltpu.CompilerParams(
            collective_id=0, has_side_effects=True, vmem_limit_bytes=48 * 1024 * 1024
        ),
    )(
        samples.reshape(rows, length),
        jnp.asarray(forward_table(length, bins)),
        jnp.asarray(inverse_table(length, LAGS, bins, padded)),
        offsets,
        bad_mask,
    )
    return tuple(jnp.transpose(x, (1, 0, 2))[:, :, :width] for x in (corr, mirr))


def solution(mesh):
    return jax.shard_map(
        on_device,
        mesh=mesh,
        in_specs=(P("blk", "rep", None), P(None, "blk"), P("blk")),
        out_specs=(P("blk", None, None), P("blk", None, None)),
        check_vma=False,
    )
```

time: 148 us -> 62.5 us (0.42)
  waiting for transfers between devices: 77 us -> 0 us
  Pallas kernels: 0 us -> 55.5 us
  local copies, waits for them, and re-layouts: 25.8 us -> 6.06 us
  other arithmetic: 13.8 us -> 0 us
  between operations: 14.2 us -> 0.65 us
  matrix products: 9.51 us -> 0 us
  starting transfers between devices: 6.78 us -> 0 us
    pallas_call x0 -> x1, Pallas kernels: none -> 55.5 us  [on_device(): pl.pallas_call(functools.partial(kernel, scale, groups), out_shape=(out,...]
    ppermute x8 -> x0, waiting for transfers between devices: 52.9 us -> none  [shifted(): lax.ppermute(x, axis, [(i, (i + by) % length) for i in range(length)])]
    psum x1 -> x0, waiting for transfers between devices: 24.1 us -> none  [on_device(): correlations = lax.psum(partial, 'rep') * scale]
    convert_element_type x4 -> x0, other arithmetic: 11.3 us -> none  [the longest x2 10 us: cross_spectrum(): second = partner.astype(jnp.float32)]
    gather x4 -> x0, local copies, waits for them, and re-layouts: 11.3 us -> none  [on_device(): partner = jnp.take(moving, offsets[stop - 1], axis=0)]
    ppermute x4 -> x0, local copies, waits for them, and re-layouts: 10 us -> none  [shifted(): lax.ppermute(x, axis, [(i, (i + by) % length) for i in range(length)])]
    dot_general x2 -> x0, matrix products: 9.51 us -> none  [the longest x1 5.93 us: on_device(): jnp.dot(samples.reshape(channels * segments, length), jnp.asarray(forward...]
    ppermute x8 -> x0, starting transfers between devices: 6.75 us -> none  [shifted(): lax.ppermute(x, axis, [(i, (i + by) % length) for i in range(length)])]
  transfers between devices with their start and end apart: 9 -> 0, of which waited for: 6 -> 0; matrix products, arithmetic and copies ran while one was open for 15% -> 0% of each run, Pallas kernels for 0% -> 0%
where the time goes in v2:
time: 62.5 us; the launch traced here: 62.3 us
  Pallas kernels  55.5 us (89%)
  local copies, waits for them, and re-layouts  6.06 us (10%)
  between operations  0.65 us (1%)
    pallas_call x1, Pallas kernels, on_device(): pl.pallas_call(functools.partial(kernel, scale, groups), out_shape=(out,...  55.5 us
    unnamed x10, local copies, waits for them, and re-layouts  6.06 us

profile of v2, /device:TPU:0, one launch (start us, length us, event | category | flops | bytes accessed | tf_op | source)
XLA Modules:
  0.0 62.3 jit_solution(5848363691611077593)
XLA Ops:
  0.6 0.0 copy-start
  0.6 1.9 %copy-done = bf16[8,2,2,128,384]{4,3,2,1,0:T(8,128)(2,1)S(1)} copy-done((bf16[8,2,2,128,384]{4,3,2,1,0:T(8,128)(2,1)S(1)}, bf16[8,2,2,128,384]{4,3,2,1,0:T(8,128)(2,1)}, u32[]{:S(2)}) %copy-start) | copy-done | bytes 3145752
  2.5 0.0 copy-start.1
  2.5 1.2 %copy-done.1 = bf16[32,8,2048]{2,1,0:T(8,128)(2,1)S(1)} copy-done((bf16[32,8,2048]{2,1,0:T(8,128)(2,1)S(1)}, bf16[32,8,2048]{2,1,0:T(8,128)(2,1)}, u32[]{:S(2)}) %copy-start.1) | copy-done | bytes 1048600
  3.7 0.0 copy-start.2
  3.8 0.7 %copy-done.2 = s32[4,32]{1,0:T(4,128)S(1)} copy-done((s32[4,32]{1,0:T(4,128)S(1)}, s32[4,32]{1,0:T(4,128)}, u32[]{:S(2)}) %copy-start.2) | copy-done | bytes 536
  4.4 0.0 copy-start.3
  4.4 0.7 %copy-done.3 = s32[32]{0:T(128)S(1)} copy-done((s32[32]{0:T(128)S(1)}, s32[32]{0:T(128)}, u32[]{:S(2)}) %copy-start.3) | copy-done | bytes 152
  5.1 55.5 %shard_map.68 = (f32[4,32,384]{2,1,0:T(8,128)S(1)}, f32[4,32,384]{2,1,0:T(8,128)S(1)}) custom-call(bf16[256,2048]{1,0:T(8,128)(2,1)S(1)} %bitcast.5, bf16[8,2048,256]{2,1,0:T(8,128)(2,1)} %constant.4.clone.table, bf16[8,2,2,128,384]{4,3,2,1,0:T(8,128)(2,1)S(1)} %copy-done, s32[4,32]{1,0:T(4,128)S(1)} %copy-done.2, s32[32]{0:T(128)S(1)} %copy-done.3), custom_call_target="tpu_custom_call" | custom-call | tf_op jit(solution)/shard_map/pallas_call | solution.py:227
  60.6 0.8 %copy.7 = f32[32,4,257]{2,1,0:T(4,128)} copy(f32[32,4,257]{2,0,1:T(8,128)S(1)} %bitcast.7) | data formatting | bytes 263168
  61.4 0.8 %copy.8 = f32[32,4,257]{2,1,0:T(4,128)} copy(f32[32,4,257]{2,0,1:T(8,128)S(1)} %bitcast.6) | data formatting | bytes 263168
Async XLA Ops:
  0.6 1.9 %copy-start = (bf16[8,2,2,128,384]{4,3,2,1,0:T(8,128)(2,1)S(1)}, bf16[8,2,2,128,384]{4,3,2,1,0:T(8,128)(2,1)}, u32[]{:S(2)}) copy-start(bf16[8,2,2,128,384]{4,3,2,1,0:T(8,128)(2,1)} %constant.5.clone.back) | copy-start | bytes 9437188
  2.5 1.2 %copy-start.1 = (bf16[32,8,2048]{2,1,0:T(8,128)(2,1)S(1)}, bf16[32,8,2048]{2,1,0:T(8,128)(2,1)}, u32[]{:S(2)}) copy-start(bf16[32,8,2048]{2,1,0:T(8,128)(2,1)} %param.5) | copy-start | bytes 3145732
  3.7 0.7 %copy-start.2 = (s32[4,32]{1,0:T(4,128)S(1)}, s32[4,32]{1,0:T(4,128)}, u32[]{:S(2)}) copy-start(s32[4,32]{1,0:T(4,128)} %offsets.1) | copy-start | bytes 1540
  4.4 0.7 %copy-start.3 = (s32[32]{0:T(128)S(1)}, s32[32]{0:T(128)}, u32[]{:S(2)}) copy-start(s32[32]{0:T(128)} %bad.1) | copy-start | bytes 388

commit v3 on v2

--- a/solution.py
+++ b/solution.py
@@ -12,6 +12,7 @@
 
 LAGS = 128
 LANES = 128
+AHEAD = 2
 MESH = pl.DeviceIdType.MESH
 F32 = jnp.float32
 BF16 = jnp.bfloat16
@@ -43,9 +44,9 @@
 def kernel(
     scale,
     groups,
-    samples, table, back, offsets, bad,
+    samples_in, table, back, offsets_in, bad_in,
     corr, mirr,
-    table_v, back_v, spec, norm, own, part, peer, even, odd_, flip,
+    samples, offsets, bad, in_sem, table_v, back_v, spec, norm, own, part, peer, even, odd_, flip,
     table_sem, back_sem, send_sem, recv_sem, rep_send, rep_recv, mir_send, mir_recv,
     *far_flat,
 ):
@@ -66,7 +67,16 @@
     def load(j):
         return pltpu.make_async_copy(table.at[j], table_v.at[j], table_sem.at[j])
 
-    for j in range(groups):
+    small = [
+        pltpu.make_async_copy(samples_in, samples, in_sem.at[0]),
+        pltpu.make_async_copy(bad_in, bad, in_sem.at[1]),
+        pltpu.make_async_copy(offsets_in, offsets, in_sem.at[2]),
+    ]
+    small[0].start()
+    load(0).start()
+    small[1].start()
+    small[2].start()
+    for j in range(1, groups):
         load(j).start()
     back_load = pltpu.make_async_copy(back, back_v, back_sem)
     back_load.start()
@@ -76,7 +86,6 @@
         for who in (lax.rem(blk + by, n), lax.rem(blk + n - by, n)):
             pl.semaphore_signal(barrier, inc=1, device_id=(who, rep), device_id_type=MESH)
     pl.semaphore_signal(barrier, inc=1, device_id=(blk, other), device_id_type=MESH)
-    pl.semaphore_wait(barrier, 2 * stops + 1)
 
     def send(src, stop, k, lane, who):
         return pltpu.make_async_remote_copy(
@@ -92,6 +101,7 @@
         send(own.at[k], stop, k, 0, up).wait_recv()
 
     norm[...] = jnp.zeros_like(norm)
+    small[0].wait()
 
     @pl.loop(0, groups)
     def _(j):
@@ -102,22 +112,29 @@
 
     power = jnp.sum(norm[...], axis=1, keepdims=True) / (groups * bins)
     norm[...] = jnp.broadcast_to(lax.rsqrt(power + 1e-06), norm.shape)
+    small[1].wait()
     for c in range(channels):
         norm[c * segs:(c + 1) * segs, :] *= (1 - bad[c]).astype(F32)
+
+    pl.semaphore_wait(barrier, 2 * stops + 1)
+
+    def launch(k):
+        send(own.at[k], 4, k, 0, up).start()
+
+        @pl.when(odd == 0)
+        def _():
+            send(own.at[k], 2, k, 1, beside).start()
+
+        @pl.when(core == 0)
+        def _():
+            send(own.at[k], 1, k, 2, sibling).start()
 
     for k in range(groups):
         real = (spec[k, :, :bins] * norm[...]).reshape(channels, segs, bins)
         imag = (spec[k, :, bins:] * norm[...]).reshape(channels, segs, bins)
         own[k] = jnp.concatenate([real, imag], axis=1).astype(BF16)
-        send(own.at[k], 4, k, 0, up).start()
-
-        @pl.when(odd == 0)
-        def _():
-            send(own.at[k], 2, k, 1, beside).start()
-
-        @pl.when(core == 0)
-        def _():
-            send(own.at[k], 1, k, 2, sibling).start()
+        if k < AHEAD:
+            launch(k)
 
     def exchange(k):
         return pltpu.make_async_remote_copy(
@@ -145,8 +162,11 @@
             )
 
     back_load.wait()
+    small[2].wait()
     for k in range(groups):
         arrived(4, k)
+        if k + AHEAD < groups:
+            launch(k + AHEAD)
 
         @pl.when(odd == 1)
         def _():
@@ -220,16 +240,19 @@
     padded = -(-width // LANES) * LANES
     scale = 1.0 / math.sqrt(segs * lax.axis_size("rep") * (length // 2))
     vmem = pl.BlockSpec(memory_space=pltpu.VMEM)
-    smem = pl.BlockSpec(memory_space=pltpu.SMEM)
     hbm = pl.BlockSpec(memory_space=pl.ANY)
     out = jax.ShapeDtypeStruct((stops, channels, padded), F32)
     dma = pltpu.SemaphoreType.DMA
     corr, mirr = pl.pallas_call(
         functools.partial(kernel, scale, groups),
         out_shape=(out, out),
-        in_specs=[vmem, hbm, hbm, smem, smem],
+        in_specs=[hbm] * 5,
         out_specs=(vmem, vmem),
         scratch_shapes=[
+            pltpu.VMEM((rows, length), BF16),
+            pltpu.SMEM((stops, channels), jnp.int32),
+            pltpu.SMEM((channels,), jnp.int32),
+            dma((3,)),
             pltpu.VMEM((groups, length, 2 * bins), BF16),
             pltpu.VMEM((groups, 2, 2, bins, padded), BF16),
             pltpu.VMEM((groups, rows, 2 * bins), F32),
@@ -246,7 +269,7 @@
             dma((stops,)), dma((stops,)),
         ] + [pltpu.VMEM((channels, 2 * segs, bins), BF16)] * (stops * groups),
         compiler_params=pltpu.CompilerParams(
-            collective_id=0, has_side_effects=True, vmem_limit_bytes=48 * 1024 * 1024
+            collective_id=0, has_side_effects=True, vmem_limit_bytes=60 * 1024 * 1024
         ),
     )(
         samples.reshape(rows, length),

time: 62.5 us -> 62.5 us (level)
  Pallas kernels: 55.5 us -> 58.2 us
  local copies, waits for them, and re-layouts: 6.06 us -> 3.46 us
    pallas_call x1, Pallas kernels: 55.5 us -> 58.2 us  [on_device(): pl.pallas_call(functools.partial(kernel, scale, groups), out_shape=(out,...]
    unnamed x10 -> x2, local copies, waits for them, and re-layouts: 6.06 us -> 3.46 us
where the time goes in v3:
time: 62.5 us; the launch traced here: 62.3 us
  Pallas kernels  58.2 us (93%)
  local copies, waits for them, and re-layouts  3.46 us (6%)
  between operations  0.64 us (1%)
    pallas_call x1, Pallas kernels, on_device(): pl.pallas_call(functools.partial(kernel, scale, groups), out_shape=(out,...  58.2 us
    unnamed x2, local copies, waits for them, and re-layouts  3.46 us

profile of v3, /device:TPU:0, one launch (start us, length us, event | category | flops | bytes accessed | tf_op | source)
XLA Modules:
  0.0 62.3 jit_solution(4075551989677385974)
XLA Ops:
  0.6 58.2 %shard_map.68 = (f32[4,32,384]{2,1,0:T(8,128)}, f32[4,32,384]{2,1,0:T(8,128)}) custom-call(bf16[256,2048]{1,0:T(8,128)(2,1)} %bitcast.5, bf16[8,2048,256]{2,1,0:T(8,128)(2,1)} %constant.4.clone.table, bf16[8,2,2,128,384]{4,3,2,1,0:T(8,128)(2,1)} %constant.5.clone.back, s32[4,32]{1,0:T(4,128)} %offsets_in.1, s32[32]{0:T(128)} %bad_in.1), custom_call_target="tpu_custom_call" | custom-call | tf_op jit(solution)/shard_map/pallas_call | solution.py:246
  58.8 1.7 %copy.7 = f32[32,4,257]{2,1,0:T(4,128)} copy(f32[32,4,257]{2,0,1:T(8,128)} %bitcast.7) | data formatting | bytes 263168
  60.6 1.7 %copy.8 = f32[32,4,257]{2,1,0:T(4,128)} copy(f32[32,4,257]{2,0,1:T(8,128)} %bitcast.6) | data formatting | bytes 263168

commit v4 on v3

--- a/solution.py
+++ b/solution.py
@@ -12,7 +12,8 @@
 
 LAGS = 128
 LANES = 128
-AHEAD = 2
+AHEAD = 3
+SUB = 8
 MESH = pl.DeviceIdType.MESH
 F32 = jnp.float32
 BF16 = jnp.bfloat16
@@ -39,6 +40,22 @@
     low = (whole - high.astype(np.float32)).astype(ml_dtypes.bfloat16)
     both = np.stack([high, low], axis=1).reshape(2, 2, -1, bins, padded)
     return np.ascontiguousarray(both.transpose(2, 0, 1, 3, 4))
+
+
+def sum_rows(tiles):
+    row = lax.broadcasted_iota(jnp.int32, tiles[0].shape, 0)
+    low = row < 4
+    tiles = [
+        jnp.where(low, tiles[i], tiles[i + 4]) + pltpu.roll(jnp.where(low, tiles[i + 4], tiles[i]), 4, 0)
+        for i in range(4)
+    ]
+    low = lax.rem(row, 4) < 2
+    tiles = [
+        jnp.where(low, tiles[i] + pltpu.roll(tiles[i], 6, 0), tiles[i + 2] + pltpu.roll(tiles[i + 2], 2, 0))
+        for i in range(2)
+    ]
+    low = lax.rem(row, 2) < 1
+    return jnp.where(low, tiles[0] + pltpu.roll(tiles[0], 7, 0), tiles[1] + pltpu.roll(tiles[1], 1, 0))
 
 
 def kernel(
@@ -149,16 +166,18 @@
     even[...] = jnp.zeros_like(even)
     odd_[...] = jnp.zeros_like(odd_)
 
-    def finish(k):
-        exchange(k).wait_recv()
+    def finish(pair):
+        first, second = 2 * pair, 2 * pair + 1
+        exchange(first).wait_recv()
+        exchange(second).wait_recv()
         for side, total in ((0, even), (1, odd_)):
-            cross = part[k, side] + peer[k, side]
+            cross = jnp.concatenate([part[k, side] + peer[k, side] for k in (first, second)], axis=1)
             high = cross.astype(BF16)
             low = (cross - high.astype(F32)).astype(BF16)
             total[...] += (
-                jnp.dot(high, back_v[k, side, 0], preferred_element_type=F32)
-                + jnp.dot(low, back_v[k, side, 0], preferred_element_type=F32)
-                + jnp.dot(high, back_v[k, side, 1], preferred_element_type=F32)
+                jnp.dot(high, back_v[pair, side, 0], preferred_element_type=F32)
+                + jnp.dot(low, back_v[pair, side, 0], preferred_element_type=F32)
+                + jnp.dot(high, back_v[pair, side, 1], preferred_element_type=F32)
             )
 
     back_load.wait()
@@ -189,23 +208,26 @@
         arrived(3, k)
         arrived(1, k)
 
-        @pl.loop(0, channels // 4)
-        def _(quad):
-            for u in range(4):
-                g = quad * 4 + u
-                mine = own[k, g].astype(F32)
-                real_a, imag_a = mine[:segs], mine[segs:]
-                for d in range(stops):
-                    theirs = far[d][k][offsets[d, g]].astype(F32)
+        @pl.loop(0, channels // SUB)
+        def _(octet):
+            base = octet * SUB
+            for d in range(stops):
+                reals, imags = [], []
+                for u in range(SUB):
+                    mine = own[k, base + u].astype(F32)
+                    theirs = far[d][k][offsets[d, base + u]].astype(F32)
+                    real_a, imag_a = mine[:segs], mine[segs:]
                     real_b, imag_b = theirs[:segs], theirs[segs:]
-                    row = pl.ds(d * channels + g, 1)
-                    part[k, 0, row, :] = jnp.sum(real_a * real_b + imag_a * imag_b, axis=0, keepdims=True)
-                    part[k, 1, row, :] = jnp.sum(imag_a * real_b - real_a * imag_b, axis=0, keepdims=True)
+                    reals.append(real_a * real_b + imag_a * imag_b)
+                    imags.append(imag_a * real_b - real_a * imag_b)
+                place = pl.ds(pl.multiple_of(d * channels + base, SUB), SUB)
+                part[k, 0, place, :] = sum_rows(reals)
+                part[k, 1, place, :] = sum_rows(imags)
 
         exchange(k).start()
-        if k >= 1:
-            finish(k - 1)
-    finish(groups - 1)
+        if k >= 2 and k % 2 == 0:
+            finish(k // 2 - 1)
+    finish(groups // 2 - 1)
 
     corr[...] = ((even[...] - odd_[...]) * scale).reshape(corr.shape)
     flip[...] = ((even[...] + odd_[...]) * scale).reshape(flip.shape)
@@ -235,13 +257,14 @@
     stops = offsets.shape[0]
     rows = channels * segs
     bins = LANES
+    assert segs == SUB and channels % SUB == 0
     groups = length // 2 // bins
     width = 2 * LAGS + 1
     padded = -(-width // LANES) * LANES
     scale = 1.0 / math.sqrt(segs * lax.axis_size("rep") * (length // 2))
     vmem = pl.BlockSpec(memory_space=pltpu.VMEM)
     hbm = pl.BlockSpec(memory_space=pl.ANY)
-    out = jax.ShapeDtypeStruct((stops, channels, padded), F32)
+    out = pltpu.VMEM((stops, channels, padded), F32)
     dma = pltpu.SemaphoreType.DMA
     corr, mirr = pl.pallas_call(
         functools.partial(kernel, scale, groups),
@@ -254,7 +277,7 @@
             pltpu.SMEM((channels,), jnp.int32),
             dma((3,)),
             pltpu.VMEM((groups, length, 2 * bins), BF16),
-            pltpu.VMEM((groups, 2, 2, bins, padded), BF16),
+            pltpu.VMEM((groups // 2, 2, 2, 2 * bins, padded), BF16),
             pltpu.VMEM((groups, rows, 2 * bins), F32),
             pltpu.VMEM((rows, bins), F32),
             pltpu.VMEM((groups, channels, 2 * segs, bins), BF16),
@@ -269,12 +292,12 @@
             dma((stops,)), dma((stops,)),
         ] + [pltpu.VMEM((channels, 2 * segs, bins), BF16)] * (stops * groups),
         compiler_params=pltpu.CompilerParams(
-            collective_id=0, has_side_effects=True, vmem_limit_bytes=60 * 1024 * 1024
+            collective_id=0, has_side_effects=True, vmem_limit_bytes=57 * 1024 * 1024
         ),
     )(
         samples.reshape(rows, length),
         jnp.asarray(forward_table(length, bins)),
-        jnp.asarray(inverse_table(length, LAGS, bins, padded)),
+        jnp.asarray(inverse_table(length, LAGS, 2 * bins, padded)),
         offsets,
         bad_mask,
     )

time: 62.5 us -> 57.2 us (0.915)
  Pallas kernels: 58.2 us -> 54.8 us
  local copies, waits for them, and re-layouts: 3.46 us -> 1.61 us
    pallas_call x1, Pallas kernels: 58.2 us -> 54.8 us  [on_device(): pl.pallas_call(functools.partial(kernel, scale, groups), out_shape=(out,...]
    unnamed x2, local copies, waits for them, and re-layouts: 3.46 us -> 1.61 us
where the time goes in v4:
time: 57.2 us; the launch traced here: 57.1 us
  Pallas kernels  54.8 us (96%)
  local copies, waits for them, and re-layouts  1.61 us (3%)
  between operations  0.64 us (1%)
    pallas_call x1, Pallas kernels, on_device(): pl.pallas_call(functools.partial(kernel, scale, groups), out_shape=(out,...  54.8 us
    unnamed x2, local copies, waits for them, and re-layouts  1.61 us

profile of v4, /device:TPU:0, one launch (start us, length us, event | category | flops | bytes accessed | tf_op | source)
XLA Modules:
  0.0 57.1 jit_solution(15391326388945384115)
XLA Ops:
  0.6 54.8 %shard_map.68 = (f32[4,32,384]{2,1,0:T(8,128)S(1)}, f32[4,32,384]{2,1,0:T(8,128)S(1)}) custom-call(bf16[256,2048]{1,0:T(8,128)(2,1)} %bitcast.7, bf16[8,2048,256]{2,1,0:T(8,128)(2,1)} %constant.4.clone.table, bf16[4,2,2,256,384]{4,3,2,1,0:T(8,128)(2,1)} %constant.5.clone.back, s32[4,32]{1,0:T(4,128)} %offsets_in.1, s32[32]{0:T(128)} %bad_in.1), custom_call_target="tpu_custom_call" | custom-call | tf_op jit(solution)/shard_map/pallas_call | solution.py:269
  55.5 0.8 %copy.7 = f32[32,4,257]{2,1,0:T(4,128)} copy(f32[32,4,257]{2,0,1:T(8,128)S(1)} %bitcast.6) | data formatting | bytes 263168
  56.3 0.8 %copy.8 = f32[32,4,257]{2,1,0:T(4,128)} copy(f32[32,4,257]{2,0,1:T(8,128)S(1)} %bitcast.5) | data formatting | bytes 263168

commit v5 on v4

--- a/solution.py
+++ b/solution.py
@@ -14,6 +14,7 @@
 LANES = 128
 AHEAD = 3
 SUB = 8
+PIECES = 4
 MESH = pl.DeviceIdType.MESH
 F32 = jnp.float32
 BF16 = jnp.bfloat16
@@ -104,18 +105,25 @@
             pl.semaphore_signal(barrier, inc=1, device_id=(who, rep), device_id_type=MESH)
     pl.semaphore_signal(barrier, inc=1, device_id=(blk, other), device_id_type=MESH)
 
-    def send(src, stop, k, lane, who):
+    def pieces(k):
+        return PIECES if k == groups - 1 else 1
+
+    def send(src, stop, k, lane, who, piece=None):
+        dst = far[stop - 1][k]
+        if piece is not None and pieces(k) > 1:
+            size = channels // PIECES
+            src, dst = (ref.at[pl.ds(piece * size, size)] for ref in (src, dst))
         return pltpu.make_async_remote_copy(
             src_ref=src,
-            dst_ref=far[stop - 1][k],
-            send_sem=send_sem.at[lane, k],
-            recv_sem=recv_sem.at[stop - 1, k],
+            dst_ref=dst,
+            send_sem=send_sem.at[lane, k, piece or 0],
+            recv_sem=recv_sem.at[stop - 1, k, piece or 0],
             device_id=(who, rep),
             device_id_type=MESH,
         )
 
-    def arrived(stop, k):
-        send(own.at[k], stop, k, 0, up).wait_recv()
+    def arrived(stop, k, piece=None):
+        send(own.at[k], stop, k, 0, up, piece).wait_recv()
 
     norm[...] = jnp.zeros_like(norm)
     small[0].wait()
@@ -136,11 +144,12 @@
     pl.semaphore_wait(barrier, 2 * stops + 1)
 
     def launch(k):
-        send(own.at[k], 4, k, 0, up).start()
-
-        @pl.when(odd == 0)
-        def _():
-            send(own.at[k], 2, k, 1, beside).start()
+        for piece in range(pieces(k)):
+            send(own.at[k], 4, k, 0, up, piece).start()
+
+            @pl.when(odd == 0)
+            def _():
+                send(own.at[k], 2, k, 1, beside, piece).start()
 
         @pl.when(core == 0)
         def _():
@@ -153,25 +162,47 @@
         if k < AHEAD:
             launch(k)
 
-    def exchange(k):
+    def exchange(k, d):
         return pltpu.make_async_remote_copy(
-            src_ref=part.at[k],
-            dst_ref=peer.at[k],
-            send_sem=rep_send.at[k],
-            recv_sem=rep_recv.at[k],
+            src_ref=part.at[k, d],
+            dst_ref=peer.at[k, d],
+            send_sem=rep_send.at[k, d],
+            recv_sem=rep_recv.at[k, d],
             device_id=(blk, other),
             device_id_type=MESH,
         )
 
+    def pair_up(k, stop):
+        d = stop - 1
+
+        @pl.loop(0, channels // SUB)
+        def _(octet):
+            base = pl.multiple_of(octet * SUB, SUB)
+            reals, imags = [], []
+            for u in range(SUB):
+                mine = own[k, base + u].astype(F32)
+                theirs = far[d][k][offsets[d, base + u]].astype(F32)
+                real_a, imag_a = mine[:segs], mine[segs:]
+                real_b, imag_b = theirs[:segs], theirs[segs:]
+                reals.append(real_a * real_b + imag_a * imag_b)
+                imags.append(imag_a * real_b - real_a * imag_b)
+            part[k, d, 0, pl.ds(base, SUB), :] = sum_rows(reals)
+            part[k, d, 1, pl.ds(base, SUB), :] = sum_rows(imags)
+
+        exchange(k, d).start()
+
     even[...] = jnp.zeros_like(even)
     odd_[...] = jnp.zeros_like(odd_)
 
     def finish(pair):
         first, second = 2 * pair, 2 * pair + 1
-        exchange(first).wait_recv()
-        exchange(second).wait_recv()
+        for d in range(stops):
+            exchange(first, d).wait_recv()
+            exchange(second, d).wait_recv()
         for side, total in ((0, even), (1, odd_)):
-            cross = jnp.concatenate([part[k, side] + peer[k, side] for k in (first, second)], axis=1)
+            cross = jnp.concatenate(
+                [(part[k, :, side] + peer[k, :, side]).reshape(stops * channels, bins) for k in (first, second)], axis=1
+            )
             high = cross.astype(BF16)
             low = (cross - high.astype(F32)).astype(BF16)
             total[...] += (
@@ -183,19 +214,22 @@
     back_load.wait()
     small[2].wait()
     for k in range(groups):
-        arrived(4, k)
-        if k + AHEAD < groups:
-            launch(k + AHEAD)
-
-        @pl.when(odd == 1)
-        def _():
-            send(far[3][k], 2, k, 1, beside).start()
+        for piece in range(pieces(k)):
+            arrived(4, k, piece)
+
+            @pl.when(odd == 1)
+            def _():
+                send(far[3][k], 2, k, 1, beside, piece).start()
 
         @pl.when(core == 1)
         def _():
             send(far[3][k], 3, k, 3, sibling).start()
 
-        arrived(2, k)
+        if k + AHEAD < groups:
+            launch(k + AHEAD)
+        pair_up(k, 4)
+        for piece in range(pieces(k)):
+            arrived(2, k, piece)
 
         @pl.when(core == 1)
         def _():
@@ -205,31 +239,14 @@
         def _():
             send(far[1][k], 3, k, 3, sibling).start()
 
-        arrived(3, k)
-        arrived(1, k)
-
-        @pl.loop(0, channels // SUB)
-        def _(octet):
-            base = octet * SUB
-            for d in range(stops):
-                reals, imags = [], []
-                for u in range(SUB):
-                    mine = own[k, base + u].astype(F32)
-                    theirs = far[d][k][offsets[d, base + u]].astype(F32)
-                    real_a, imag_a = mine[:segs], mine[segs:]
-                    real_b, imag_b = theirs[:segs], theirs[segs:]
-                    reals.append(real_a * real_b + imag_a * imag_b)
-                    imags.append(imag_a * real_b - real_a * imag_b)
-                place = pl.ds(pl.multiple_of(d * channels + base, SUB), SUB)
-                part[k, 0, place, :] = sum_rows(reals)
-                part[k, 1, place, :] = sum_rows(imags)
-
-        exchange(k).start()
+        pair_up(k, 2)
+        for stop in (3, 1):
+            arrived(stop, k)
+            pair_up(k, stop)
         if k >= 2 and k % 2 == 0:
             finish(k // 2 - 1)
     finish(groups // 2 - 1)
 
-    corr[...] = ((even[...] - odd_[...]) * scale).reshape(corr.shape)
     flip[...] = ((even[...] + odd_[...]) * scale).reshape(flip.shape)
     back_home = [
         pltpu.make_async_remote_copy(
@@ -244,10 +261,13 @@
     ]
     for copy in back_home:
         copy.start()
+    corr[...] = ((even[...] - odd_[...]) * scale).reshape(corr.shape)
     for k in range(groups):
         for lane in range(4):
-            send(own.at[k], 4, k, lane, up).wait_send()
-        exchange(k).wait_send()
+            for piece in range(pieces(k) if lane < 2 else 1):
+                send(own.at[k], 4, k, lane, up, piece if lane < 2 else None).wait_send()
+        for d in range(stops):
+            exchange(k, d).wait_send()
     for copy in back_home:
         copy.wait()
 
@@ -281,14 +301,14 @@
             pltpu.VMEM((groups, rows, 2 * bins), F32),
             pltpu.VMEM((rows, bins), F32),
             pltpu.VMEM((groups, channels, 2 * segs, bins), BF16),
-            pltpu.VMEM((groups, 2, stops * channels, bins), F32),
-            pltpu.VMEM((groups, 2, stops * channels, bins), F32),
+            pltpu.VMEM((groups, stops, 2, channels, bins), F32),
+            pltpu.VMEM((groups, stops, 2, channels, bins), F32),
             pltpu.VMEM((stops * channels, padded), F32),
             pltpu.VMEM((stops * channels, padded), F32),
             pltpu.VMEM((stops, channels, padded), F32),
             dma((groups,)), dma,
-            dma((4, groups)), dma((stops, groups)),
-            dma((groups,)), dma((groups,)),
+            dma((4, groups, PIECES)), dma((stops, groups, PIECES)),
+            dma((groups, stops)), dma((groups, stops)),
             dma((stops,)), dma((stops,)),
         ] + [pltpu.VMEM((channels, 2 * segs, bins), BF16)] * (stops * groups),
         compiler_params=pltpu.CompilerParams(

time: 57.2 us -> 55.6 us (0.972)
  Pallas kernels: 54.8 us -> 53.2 us
    pallas_call x1, Pallas kernels: 54.8 us -> 53.2 us  [on_device(): pl.pallas_call(functools.partial(kernel, scale, groups), out_shape=(out,...]
where the time goes in v5:
time: 55.6 us; the launch traced here: 55.5 us
  Pallas kernels  53.2 us (96%)
  local copies, waits for them, and re-layouts  1.61 us (3%)
  between operations  0.64 us (1%)
    pallas_call x1, Pallas kernels, on_device(): pl.pallas_call(functools.partial(kernel, scale, groups), out_shape=(out,...  53.2 us
    unnamed x2, local copies, waits for them, and re-layouts  1.61 us

profile of v5, /device:TPU:0, one launch (start us, length us, event | category | flops | bytes accessed | tf_op | source)
XLA Modules:
  0.0 55.5 jit_solution(13199429329007106971)
XLA Ops:
  0.6 53.2 %shard_map.68 = (f32[4,32,384]{2,1,0:T(8,128)S(1)}, f32[4,32,384]{2,1,0:T(8,128)S(1)}) custom-call(bf16[256,2048]{1,0:T(8,128)(2,1)} %bitcast.7, bf16[8,2048,256]{2,1,0:T(8,128)(2,1)} %constant.4.clone.table, bf16[4,2,2,256,384]{4,3,2,1,0:T(8,128)(2,1)} %constant.5.clone.back, s32[4,32]{1,0:T(4,128)} %offsets_in.1, s32[32]{0:T(128)} %bad_in.1), custom_call_target="tpu_custom_call" | custom-call | tf_op jit(solution)/shard_map/pallas_call | solution.py:289
  53.9 0.8 %copy.7 = f32[32,4,257]{2,1,0:T(4,128)} copy(f32[32,4,257]{2,0,1:T(8,128)S(1)} %bitcast.6) | data formatting | bytes 263168
  54.7 0.8 %copy.8 = f32[32,4,257]{2,1,0:T(4,128)} copy(f32[32,4,257]{2,0,1:T(8,128)S(1)} %bitcast.5) | data formatting | bytes 263168

commit v6 on v5

--- a/solution.py
+++ b/solution.py
@@ -97,7 +97,6 @@
     for j in range(1, groups):
         load(j).start()
     back_load = pltpu.make_async_copy(back, back_v, back_sem)
-    back_load.start()
 
     barrier = pltpu.get_barrier_semaphore()
     for by in range(1, stops + 1):
@@ -135,6 +134,7 @@
         spec[j] = got
         norm[...] += got[:, :bins] * got[:, :bins] + got[:, bins:] * got[:, bins:]
 
+    back_load.start()
     power = jnp.sum(norm[...], axis=1, keepdims=True) / (groups * bins)
     norm[...] = jnp.broadcast_to(lax.rsqrt(power + 1e-06), norm.shape)
     small[1].wait()
@@ -194,62 +194,32 @@
     even[...] = jnp.zeros_like(even)
     odd_[...] = jnp.zeros_like(odd_)
 
-    def finish(pair):
+    def finish(pair, stops_done):
         first, second = 2 * pair, 2 * pair + 1
-        for d in range(stops):
+        low_d, high_d = min(stops_done) - 1, max(stops_done)
+        for d in range(low_d, high_d):
             exchange(first, d).wait_recv()
             exchange(second, d).wait_recv()
+        count = (high_d - low_d) * channels
+        held = pl.ds(low_d * channels, count)
         for side, total in ((0, even), (1, odd_)):
             cross = jnp.concatenate(
-                [(part[k, :, side] + peer[k, :, side]).reshape(stops * channels, bins) for k in (first, second)], axis=1
+                [
+                    (part[k, low_d:high_d, side] + peer[k, low_d:high_d, side]).reshape(count, bins)
+                    for k in (first, second)
+                ],
+                axis=1,
             )
             high = cross.astype(BF16)
             low = (cross - high.astype(F32)).astype(BF16)
-            total[...] += (
+            total[held, :] += (
                 jnp.dot(high, back_v[pair, side, 0], preferred_element_type=F32)
                 + jnp.dot(low, back_v[pair, side, 0], preferred_element_type=F32)
                 + jnp.dot(high, back_v[pair, side, 1], preferred_element_type=F32)
             )
 
-    back_load.wait()
-    small[2].wait()
-    for k in range(groups):
-        for piece in range(pieces(k)):
-            arrived(4, k, piece)
-
-            @pl.when(odd == 1)
-            def _():
-                send(far[3][k], 2, k, 1, beside, piece).start()
-
-        @pl.when(core == 1)
-        def _():
-            send(far[3][k], 3, k, 3, sibling).start()
-
-        if k + AHEAD < groups:
-            launch(k + AHEAD)
-        pair_up(k, 4)
-        for piece in range(pieces(k)):
-            arrived(2, k, piece)
-
-        @pl.when(core == 1)
-        def _():
-            send(far[1][k], 1, k, 2, sibling).start()
-
-        @pl.when(core == 0)
-        def _():
-            send(far[1][k], 3, k, 3, sibling).start()
-
-        pair_up(k, 2)
-        for stop in (3, 1):
-            arrived(stop, k)
-            pair_up(k, stop)
-        if k >= 2 and k % 2 == 0:
-            finish(k // 2 - 1)
-    finish(groups // 2 - 1)
-
-    flip[...] = ((even[...] + odd_[...]) * scale).reshape(flip.shape)
-    back_home = [
-        pltpu.make_async_remote_copy(
+    def go_home(d):
+        return pltpu.make_async_remote_copy(
             src_ref=flip.at[d],
             dst_ref=mirr.at[d],
             send_sem=mir_send.at[d],
@@ -257,19 +227,61 @@
             device_id=(lax.rem(blk + n - d - 1, n), rep),
             device_id_type=MESH,
         )
-        for d in range(stops)
-    ]
-    for copy in back_home:
-        copy.start()
-    corr[...] = ((even[...] - odd_[...]) * scale).reshape(corr.shape)
+
+    def conclude(stop):
+        d = stop - 1
+        finish(groups // 2 - 1, (stop,))
+        held = pl.ds(d * channels, channels)
+        flip[d] = (even[held, :] + odd_[held, :]) * scale
+        go_home(d).start()
+        corr[d] = (even[held, :] - odd_[held, :]) * scale
+
+    back_load.wait()
+    small[2].wait()
+    for k in range(groups):
+        for piece in range(pieces(k)):
+            arrived(4, k, piece)
+
+            @pl.when(odd == 1)
+            def _():
+                send(far[3][k], 2, k, 1, beside, piece).start()
+
+        @pl.when(core == 1)
+        def _():
+            send(far[3][k], 3, k, 3, sibling).start()
+
+        if k + AHEAD < groups:
+            launch(k + AHEAD)
+        pair_up(k, 4)
+        for piece in range(pieces(k)):
+            arrived(2, k, piece)
+
+        @pl.when(core == 1)
+        def _():
+            send(far[1][k], 1, k, 2, sibling).start()
+
+        @pl.when(core == 0)
+        def _():
+            send(far[1][k], 3, k, 3, sibling).start()
+
+        pair_up(k, 2)
+        for stop in (3, 1):
+            arrived(stop, k)
+            pair_up(k, stop)
+            if k == groups - 1:
+                conclude(4 if stop == 3 else 2)
+        if k >= 2 and k % 2 == 0:
+            finish(k // 2 - 1, range(1, stops + 1))
+    conclude(3)
+    conclude(1)
     for k in range(groups):
         for lane in range(4):
             for piece in range(pieces(k) if lane < 2 else 1):
                 send(own.at[k], 4, k, lane, up, piece if lane < 2 else None).wait_send()
         for d in range(stops):
             exchange(k, d).wait_send()
-    for copy in back_home:
-        copy.wait()
+    for d in range(stops):
+        go_home(d).wait()
 
 
 def on_device(samples, offsets, bad_mask):

time: 55.6 us -> 54.8 us (0.986)
  Pallas kernels: 53.2 us -> 52.4 us
    pallas_call x1, Pallas kernels: 53.2 us -> 52.4 us  [on_device(): pl.pallas_call(functools.partial(kernel, scale, groups), out_shape=(out,...]
where the time goes in v6:
time: 54.8 us; the launch traced here: 54.7 us
  Pallas kernels  52.4 us (96%)
  local copies, waits for them, and re-layouts  1.61 us (3%)
  between operations  0.64 us (1%)
    pallas_call x1, Pallas kernels, on_device(): pl.pallas_call(functools.partial(kernel, scale, groups), out_shape=(out,...  52.4 us
    unnamed x2, local copies, waits for them, and re-layouts  1.61 us

profile of v6, /device:TPU:0, one launch (start us, length us, event | category | flops | bytes accessed | tf_op | source)
XLA Modules:
  0.0 54.7 jit_solution(18293285792549110914)
XLA Ops:
  0.6 52.4 %shard_map.68 = (f32[4,32,384]{2,1,0:T(8,128)S(1)}, f32[4,32,384]{2,1,0:T(8,128)S(1)}) custom-call(bf16[256,2048]{1,0:T(8,128)(2,1)} %bitcast.7, bf16[8,2048,256]{2,1,0:T(8,128)(2,1)} %constant.4.clone.table, bf16[4,2,2,256,384]{4,3,2,1,0:T(8,128)(2,1)} %constant.5.clone.back, s32[4,32]{1,0:T(4,128)} %offsets_in.1, s32[32]{0:T(128)} %bad_in.1), custom_call_target="tpu_custom_call" | custom-call | tf_op jit(solution)/shard_map/pallas_call | solution.py:301
  53.1 0.8 %copy.7 = f32[32,4,257]{2,1,0:T(4,128)} copy(f32[32,4,257]{2,0,1:T(8,128)S(1)} %bitcast.6) | data formatting | bytes 263168
  53.9 0.8 %copy.8 = f32[32,4,257]{2,1,0:T(4,128)} copy(f32[32,4,257]{2,0,1:T(8,128)S(1)} %bitcast.5) | data formatting | bytes 263168

commit v7 on v6

--- a/solution.py
+++ b/solution.py
@@ -25,7 +25,7 @@
     angle = phase * (2.0 * math.pi / length)
     real = np.cos(angle).reshape(length, -1, bins)
     imag = -np.sin(angle).reshape(length, -1, bins)
-    both = np.concatenate([real, imag], axis=2).transpose(1, 0, 2)
+    both = np.concatenate([real, imag], axis=2).reshape(length, -1, 4 * bins).transpose(1, 0, 2)
     return np.ascontiguousarray(both).astype(ml_dtypes.bfloat16)
 
 
@@ -94,7 +94,7 @@
     load(0).start()
     small[1].start()
     small[2].start()
-    for j in range(1, groups):
+    for j in range(1, groups // 2):
         load(j).start()
     back_load = pltpu.make_async_copy(back, back_v, back_sem)
 
@@ -105,12 +105,12 @@
     pl.semaphore_signal(barrier, inc=1, device_id=(blk, other), device_id_type=MESH)
 
     def pieces(k):
-        return PIECES if k == groups - 1 else 1
+        return PIECES if k == groups - 1 else PIECES // 2
 
     def send(src, stop, k, lane, who, piece=None):
         dst = far[stop - 1][k]
         if piece is not None and pieces(k) > 1:
-            size = channels // PIECES
+            size = channels // pieces(k)
             src, dst = (ref.at[pl.ds(piece * size, size)] for ref in (src, dst))
         return pltpu.make_async_remote_copy(
             src_ref=src,
@@ -127,12 +127,14 @@
     norm[...] = jnp.zeros_like(norm)
     small[0].wait()
 
-    @pl.loop(0, groups)
+    @pl.loop(0, groups // 2)
     def _(j):
         load(j).wait()
         got = jnp.dot(samples[...], table_v[j], preferred_element_type=F32)
-        spec[j] = got
-        norm[...] += got[:, :bins] * got[:, :bins] + got[:, bins:] * got[:, bins:]
+        spec[2 * j] = got[:, :2 * bins]
+        spec[2 * j + 1] = got[:, 2 * bins:]
+        square = got * got
+        norm[...] += (square[:, :bins] + square[:, bins:2 * bins]) + (square[:, 2 * bins:3 * bins] + square[:, 3 * bins:])
 
     back_load.start()
     power = jnp.sum(norm[...], axis=1, keepdims=True) / (groups * bins)
@@ -308,7 +310,7 @@
             pltpu.SMEM((stops, channels), jnp.int32),
             pltpu.SMEM((channels,), jnp.int32),
             dma((3,)),
-            pltpu.VMEM((groups, length, 2 * bins), BF16),
+            pltpu.VMEM((groups // 2, length, 4 * bins), BF16),
             pltpu.VMEM((groups // 2, 2, 2, 2 * bins, padded), BF16),
             pltpu.VMEM((groups, rows, 2 * bins), F32),
             pltpu.VMEM((rows, bins), F32),
@@ -318,7 +320,7 @@
             pltpu.VMEM((stops * channels, padded), F32),
             pltpu.VMEM((stops * channels, padded), F32),
             pltpu.VMEM((stops, channels, padded), F32),
-            dma((groups,)), dma,
+            dma((groups // 2,)), dma,
             dma((4, groups, PIECES)), dma((stops, groups, PIECES)),
             dma((groups, stops)), dma((groups, stops)),
             dma((stops,)), dma((stops,)),

time: 54.8 us -> 53.1 us (0.969)
  Pallas kernels: 52.4 us -> 50.7 us
    pallas_call x1, Pallas kernels: 52.4 us -> 50.7 us  [on_device(): pl.pallas_call(functools.partial(kernel, scale, groups), out_shape=(out,...]
where the time goes in v7:
time: 53.1 us; the launch traced here: 52.9 us
  Pallas kernels  50.7 us (95%)
  local copies, waits for them, and re-layouts  1.61 us (3%)
  between operations  0.64 us (1%)
    pallas_call x1, Pallas kernels, on_device(): pl.pallas_call(functools.partial(kernel, scale, groups), out_shape=(out,...  50.7 us
    unnamed x2, local copies, waits for them, and re-layouts  1.61 us

profile of v7, /device:TPU:0, one launch (start us, length us, event | category | flops | bytes accessed | tf_op | source)
XLA Modules:
  0.0 52.9 jit_solution(13442272161676201440)
XLA Ops:
  0.6 50.7 %shard_map.68 = (f32[4,32,384]{2,1,0:T(8,128)S(1)}, f32[4,32,384]{2,1,0:T(8,128)S(1)}) custom-call(bf16[256,2048]{1,0:T(8,128)(2,1)} %bitcast.7, bf16[4,2048,512]{2,1,0:T(8,128)(2,1)} %constant.4.clone.table, bf16[4,2,2,256,384]{4,3,2,1,0:T(8,128)(2,1)} %constant.5.clone.back, s32[4,32]{1,0:T(4,128)} %offsets_in.1, s32[32]{0:T(128)} %bad_in.1), custom_call_target="tpu_custom_call" | custom-call | tf_op jit(solution)/shard_map/pallas_call | solution.py:303
  51.3 0.8 %copy.7 = f32[32,4,257]{2,1,0:T(4,128)} copy(f32[32,4,257]{2,0,1:T(8,128)S(1)} %bitcast.6) | data formatting | bytes 263168
  52.1 0.8 %copy.8 = f32[32,4,257]{2,1,0:T(4,128)} copy(f32[32,4,257]{2,0,1:T(8,128)S(1)} %bitcast.5) | data formatting | bytes 263168

commit v8 on v7

--- a/solution.py
+++ b/solution.py
@@ -12,7 +12,7 @@
 
 LAGS = 128
 LANES = 128
-AHEAD = 3
+AHEAD = 4
 SUB = 8
 PIECES = 4
 MESH = pl.DeviceIdType.MESH
@@ -127,7 +127,7 @@
     norm[...] = jnp.zeros_like(norm)
     small[0].wait()
 
-    @pl.loop(0, groups // 2)
+    @pl.loop(0, groups // 2, unroll=True)
     def _(j):
         load(j).wait()
         got = jnp.dot(samples[...], table_v[j], preferred_element_type=F32)
@@ -241,6 +241,8 @@
     back_load.wait()
     small[2].wait()
     for k in range(groups):
+        if k + AHEAD < groups:
+            launch(k + AHEAD)
         for piece in range(pieces(k)):
             arrived(4, k, piece)
 
@@ -252,8 +254,6 @@
         def _():
             send(far[3][k], 3, k, 3, sibling).start()
 
-        if k + AHEAD < groups:
-            launch(k + AHEAD)
         pair_up(k, 4)
         for piece in range(pieces(k)):
             arrived(2, k, piece)

time: 53.1 us -> 53.4 us (level)
  no operation moved by 1% of the time
where the time goes in v8:
time: 53.4 us; the launch traced here: 53.2 us
  Pallas kernels  51 us (96%)
  local copies, waits for them, and re-layouts  1.61 us (3%)
  between operations  0.64 us (1%)
    pallas_call x1, Pallas kernels, on_device(): pl.pallas_call(functools.partial(kernel, scale, groups), out_shape=(out,...  51 us
    unnamed x2, local copies, waits for them, and re-layouts  1.61 us

profile of v8, /device:TPU:0, one launch (start us, length us, event | category | flops | bytes accessed | tf_op | source)
XLA Modules:
  0.0 53.2 jit_solution(3883458759333989911)
XLA Ops:
  0.6 51.0 %shard_map.68 = (f32[4,32,384]{2,1,0:T(8,128)S(1)}, f32[4,32,384]{2,1,0:T(8,128)S(1)}) custom-call(bf16[256,2048]{1,0:T(8,128)(2,1)} %bitcast.7, bf16[4,2048,512]{2,1,0:T(8,128)(2,1)} %constant.4.clone.table, bf16[4,2,2,256,384]{4,3,2,1,0:T(8,128)(2,1)} %constant.5.clone.back, s32[4,32]{1,0:T(4,128)} %offsets_in.1, s32[32]{0:T(128)} %bad_in.1), custom_call_target="tpu_custom_call" | custom-call | tf_op jit(solution)/shard_map/pallas_call | solution.py:303
  51.6 0.8 %copy.7 = f32[32,4,257]{2,1,0:T(4,128)} copy(f32[32,4,257]{2,0,1:T(8,128)S(1)} %bitcast.6) | data formatting | bytes 263168
  52.4 0.8 %copy.8 = f32[32,4,257]{2,1,0:T(4,128)} copy(f32[32,4,257]{2,0,1:T(8,128)S(1)} %bitcast.5) | data formatting | bytes 263168

commit v9 on v8

--- a/solution.py
+++ b/solution.py
@@ -105,7 +105,7 @@
     pl.semaphore_signal(barrier, inc=1, device_id=(blk, other), device_id_type=MESH)
 
     def pieces(k):
-        return PIECES if k == groups - 1 else PIECES // 2
+        return PIECES
 
     def send(src, stop, k, lane, who, piece=None):
         dst = far[stop - 1][k]

time: 53.4 us -> 53.4 us (level)
  no operation moved by 1% of the time
where the time goes in v9:
time: 53.4 us; the launch traced here: 53.2 us
  Pallas kernels  51 us (96%)
  local copies, waits for them, and re-layouts  1.61 us (3%)
  between operations  0.64 us (1%)
    pallas_call x1, Pallas kernels, on_device(): pl.pallas_call(functools.partial(kernel, scale, groups), out_shape=(out,...  51 us
    unnamed x2, local copies, waits for them, and re-layouts  1.61 us

profile of v9, /device:TPU:0, one launch (start us, length us, event | category | flops | bytes accessed | tf_op | source)
XLA Modules:
  0.0 53.2 jit_solution(349111443493623609)
XLA Ops:
  0.6 51.0 %shard_map.68 = (f32[4,32,384]{2,1,0:T(8,128)S(1)}, f32[4,32,384]{2,1,0:T(8,128)S(1)}) custom-call(bf16[256,2048]{1,0:T(8,128)(2,1)} %bitcast.7, bf16[4,2048,512]{2,1,0:T(8,128)(2,1)} %constant.4.clone.table, bf16[4,2,2,256,384]{4,3,2,1,0:T(8,128)(2,1)} %constant.5.clone.back, s32[4,32]{1,0:T(4,128)} %offsets_in.1, s32[32]{0:T(128)} %bad_in.1), custom_call_target="tpu_custom_call" | custom-call | tf_op jit(solution)/shard_map/pallas_call | solution.py:303
  51.6 0.8 %copy.7 = f32[32,4,257]{2,1,0:T(4,128)} copy(f32[32,4,257]{2,0,1:T(8,128)S(1)} %bitcast.6) | data formatting | bytes 263168
  52.4 0.8 %copy.8 = f32[32,4,257]{2,1,0:T(4,128)} copy(f32[32,4,257]{2,0,1:T(8,128)S(1)} %bitcast.5) | data formatting | bytes 263168
